TPU v7x, 512 devices: a whole 4x4x16 slice. The times are simulated.
512 devices in a mesh: lat: 16 (over x, y_hi, core), lon: 32 (over z, y_lo).
Axes of the slice: x: 4, y: 4 (y_hi: 2, y_lo: 2; y = y_hi * 2 + y_lo), z: 16, core: 2. Of those that a mesh axis runs over, the one named last changes fastest.
Arguments:
- tracer: float32 [8, 256, 36864], P(None, 'lat', 'lon'), may hold values from -6 to 6
- flux: float32 [256, 36864], P('lat', 'lon'), may hold values from -6 to 6
- winds: float32 [3, 8, 256, 768], P(None, None, 'lat', 'lon'), may hold values from -0.3 to 0.3
- obs_cells: int32 [8192, 3], P(('lat', 'lon')), may hold values from 0 to 767, as said below
- obs_count: int32 [512], P(('lat', 'lon')), may hold values from 1 to 16, as said below
- obs_value: float32 [8192], P(('lat', 'lon')), may hold values from -6 to 6
- obs_var: float32 [8192], P(('lat', 'lon')), may hold values from 21.333334 to 341.33334
Outputs:
- tracer_out: float32 [8, 256, 36864], P(None, 'lat', 'lon')
- flux_out: float32 [256, 36864], P('lat', 'lon')
Inputs may be any that keep to these rules, and one draw needn't show every extreme that they name: `obs_cells`: slot k lies in the block of 16 slots of device k div 16 (devices in lat-major order), and its cell lies in that device's block of the grid: row in its 16 rows, column in its 24 columns, level below 8. Each device's first slot is the last row, last column and highest level of its block, its second slot the first row, first column and level 0 of its block. Cells may repeat. Live slots are the first obs_count of each device's slots; some device has all 16 slots live.
All inputs are finite; a program needn't handle non-finite values.
Results may differ from a plain program's by a relative error of at most 0.0001.
Values sent between devices are 32-bit elements; how exact they have to be, the bound alone decides.
A program may use at most 64 MiB of HBM per device.

v0:
```python
import jax
import jax.numpy as jnp
from jax import lax
from jax.sharding import PartitionSpec as P

M = 48
NS_ITERS = 5


KH = 0.15


def with_halo(value, sides, width, wrap):
    for axis, dim in sides:
        size, length = (lax.axis_size(axis), value.shape[dim])
        up = [(i, (i + 1) % size) for i in range(size if wrap else size - 1)]
        down = [(j, i) for i, j in up]
        last = lax.slice_in_dim(value, length - width, length, axis=dim)
        leading = lax.slice_in_dim(value, 0, width, axis=dim)
        before = lax.ppermute(last, axis, up)
        after = lax.ppermute(leading, axis, down)
        value = jnp.concatenate([before, value, after], axis=dim)
    return value


def advance(center, lat_minus, lat_plus, lon_prev, lon_next, wind_u, wind_v, wind_w):
    zeros = jnp.zeros_like(center[:1])
    above = jnp.concatenate([center[1:], zeros], axis=0)
    below = jnp.concatenate([zeros, center[:-1]], axis=0)
    result = (
        center - 0.5 * wind_u * (lon_next - lon_prev) + KH * (lon_next - 2.0 * center + lon_prev)
    )
    result = (
        result - 0.5 * wind_v * (lat_plus - lat_minus) + KH * (lat_plus - 2.0 * center + lat_minus)
    )
    result = result - 0.5 * wind_w * (above - below) + KH * (above - 2.0 * center + below)
    return result


def member_transform(gram, proj, members):
    eye = jnp.eye(members, dtype=jnp.float32)
    hp = lax.Precision.HIGHEST
    system = (members - 1.0) * eye + gram
    scale = jnp.sqrt(jnp.sum(system * system))
    root_now = system / scale
    inverse_now = eye
    for step in range(NS_ITERS):
        factor = 0.5 * (3.0 * eye - jnp.dot(inverse_now, root_now, precision=hp))
        root_now = jnp.dot(root_now, factor, precision=hp)
        inverse_now = jnp.dot(factor, inverse_now, precision=hp)
    wmean = jnp.dot(inverse_now, jnp.dot(inverse_now, proj, precision=hp), precision=hp) / scale
    root = jnp.sqrt((members - 1.0) / scale) * inverse_now
    centering = eye - 1.0 / members
    return jnp.dot(centering, wmean[:, None] + root, precision=hp) + 1.0 / members


def as_members(flat, columns):
    return flat.reshape(flat.shape[0], flat.shape[1], columns, M)


def advance_flat(center, lat_minus, lat_plus, lon_prev, lon_next, wind_block):
    columns = wind_block.shape[-1]
    result = advance(
        as_members(center, columns),
        as_members(lat_minus, columns),
        as_members(lat_plus, columns),
        as_members(lon_prev, columns),
        as_members(lon_next, columns),
        wind_block[0][..., None],
        wind_block[1][..., None],
        wind_block[2][..., None],
    )
    return result.reshape(center.shape)


def shallow_step(field, winds):
    lon_wide = with_halo(field, (("lon", 2),), M, True)
    lat_wide = with_halo(field, (("lat", 1),), 1, False)
    return advance_flat(
        field,
        lat_wide[:, :-2],
        lat_wide[:, 2:],
        lon_wide[:, :, : -2 * M],
        lon_wide[:, :, 2 * M :],
        winds,
    )


def on_device(tracer, flux, winds, obs_cells, obs_count, obs_value, obs_var):
    hp = lax.Precision.HIGHEST
    levels, rows, width = tracer.shape
    columns = width // M
    field = tracer.at[0].add(flux)
    field = shallow_step(field, winds)
    field = shallow_step(field, winds)
    row_local = obs_cells[:, 0] - lax.axis_index("lat") * rows
    col_local = obs_cells[:, 1] - lax.axis_index("lon") * columns
    flat_index = (obs_cells[:, 2] * rows + row_local) * columns + col_local
    member_rows = field.reshape(-1, M)
    observed = jnp.take(member_rows, flat_index, axis=0)
    slots = obs_value.shape[0]
    live = (jnp.arange(slots, dtype=jnp.int32) < obs_count[0]).astype(jnp.float32)
    hbar = jnp.mean(observed, axis=1)
    anomalies = observed - hbar[:, None]
    weight = live / obs_var
    weighted_innov = weight * (obs_value - hbar)
    gram_part = jnp.dot(anomalies.T * weight[None, :], anomalies, precision=hp)
    proj_part = jnp.dot(anomalies.T, weighted_innov, precision=hp)
    gram, proj = lax.psum((gram_part, proj_part), ("lat", "lon"))
    mixing = member_transform(gram, proj, M)
    tracer_out = jnp.dot(member_rows, mixing, precision=hp).reshape(levels, rows, width)
    flux_out = jnp.dot(flux.reshape(-1, M), mixing, precision=hp).reshape(rows, width)
    return (tracer_out, flux_out)


def solution(mesh):
    return jax.shard_map(
        on_device,
        mesh=mesh,
        in_specs=(
            P(None, "lat", "lon"),
            P("lat", "lon"),
            P(None, None, "lat", "lon"),
            P(("lat", "lon"), None),
            P(("lat", "lon")),
            P(("lat", "lon")),
            P(("lat", "lon")),
        ),
        out_specs=(P(None, "lat", "lon"), P("lat", "lon")),
        check_vma=False,
    )
```

profile of v0, /device:TPU:1, one launch (start us, length us, event | category | flops | bytes accessed | tf_op | source)
XLA Modules:
  0.0 195.2 jit_solution(5435071610383970742)
XLA Ops:
  3.3 13.0 %collective-permute-start = (f32[8,16,48]{2,1,0:T(8,128)}, f32[8,16,48]{2,1,0:T(8,128)S(1)}, u32[]{:S(2)}, u32[]{:S(2)}) collective-permute-start(f32[8,16,48]{2,1,0:T(8,128)} %get-tuple-element.32), channel_id=1, source_target_pairs={{1,0},{2,1},{3,2},{4,3},{5,4},{6,5},{7,6},{8,7},{9,8},{10,9},{11,1... | collective-permute-start | bytes 73736 | tf_op jit(solution)/shard_map/ppermute | solution.py:21
  16.2 1.9 collective-permute-start.1
  18.9 2.9 %collective-permute-start.2 = (f32[8,1,1152]{2,1,0:T(1,128)}, f32[8,1,1152]{2,1,0:T(1,128)}, u32[]{:S(2)}, u32[]{:S(2)}) collective-permute-start(f32[8,1,1152]{2,1,0:T(1,128)} %get-tuple-element.34), channel_id=1, source_target_pairs={{32,0},{64,32},{96,64},{128,96},{160,128},{192,160},{224,192},{256... | collective-permute-start | bytes 110600 | tf_op jit(solution)/shard_map/ppermute | solution.py:21
  21.7 4.4 %collective-permute-start.3 = (f32[8,1,1152]{2,1,0:T(1,128)}, f32[8,1,1152]{2,1,0:T(1,128)}, u32[]{:S(2)}, u32[]{:S(2)}) collective-permute-start(f32[8,1,1152]{2,1,0:T(1,128)} %get-tuple-element.35), channel_id=1, source_target_pairs={{0,32},{32,64},{64,96},{96,128},{128,160},{160,192},{192,224},{224... | collective-permute-start | bytes 110600 | tf_op jit(solution)/shard_map/ppermute | solution.py:20
  28.0 2.8 %slice.130 = f32[7,16,24,48]{3,2,1,0:T(8,128)} reshape(f32[7,16,1152]{2,1,0:T(8,128)} %get-tuple-element.36) | data formatting | bytes 1032192 | tf_op jit(solution)/shard_map/slice | solution.py:28
  30.8 1.7 slice.132
  33.2 2.4 %pad_maximum_fusion.7 = (f32[8,16,1152]{2,1,0:T(8,128)}, f32[8,16,1152]{2,1,0:T(8,128)}, f32[8,16,1152]{2,1,0:T(8,128)}, f32[8,16,1152]{2,1,0:T(8,128)S(1)}) fusion(f32[8,16,48]{2,1,0:T(8,128)S(1)} %collective-permute-done, f32[8,16,1152]{2,1,0:T(8,128)S(1)} %fusion.14, f32[8,16,48]{2,1,0:T(8,128)S(1)} %collective-permute-done.1, ...), kind=kLoop, calls=%fused_computation.38 | loop fusion | flops 589824 | bytes 3072000 | tf_op jit(solution)/shard_map/concatenate | solution.py:22
  35.5 2.9 %reshape.116 = f32[8,16,24,48]{3,2,1,0:T(8,128)} reshape(f32[8,16,1152]{2,1,0:T(8,128)} %get-tuple-element.28) | data formatting | bytes 1179648 | tf_op jit(solution)/shard_map/reshape | solution.py:58
  38.4 2.9 %reshape.117 = f32[8,16,24,48]{3,2,1,0:T(8,128)} reshape(f32[8,16,1152]{2,1,0:T(8,128)} %get-tuple-element.29) | data formatting | bytes 1179648 | tf_op jit(solution)/shard_map/reshape | solution.py:58
  41.4 1.8 reshape.118
  43.2 1.8 reshape.119
  45.0 4.8 %fusion.2 = f32[8,16,24,48]{3,2,1,0:T(8,128)S(1)} fusion(f32[7,16,24,48]{3,2,1,0:T(8,128)} %slice.132, f32[7,16,24,48]{3,2,1,0:T(8,128)} %slice.130, f32[8,16,24,48]{3,2,1,0:T(8,128)} %reshape.119, f32[8,16,24,48]{3,2,1,0:T(8,128)} %reshape.118, f32[8,16,24,48]{3,2,1,0:T(8,128)} %reshape.117, f32[8,16,24,48]{3,2,1,0:T(8,128)} %reshape.116, ...), kind=kLoop, calls=%fused_computation.9 | loop fusion | flops 3244032 | bytes 4608000 | tf_op jit(solution)/shard_map/add | solution.py:36
  50.5 5.2 %collective-permute-start.4 = (f32[8,16,48]{2,1,0:T(8,128)S(1)}, f32[8,16,48]{2,1,0:T(8,128)S(1)}, u32[]{:S(2)}, u32[]{:S(2)}) collective-permute-start(f32[8,16,48]{2,1,0:T(8,128)S(1)} %get-tuple-element.24), channel_id=1, source_target_pairs={{1,0},{2,1},{3,2},{4,3},{5,4},{6,5},{7,6},{8,7},{9,8},{10,9},{11,1... | collective-permute-start | bytes 73736 | tf_op jit(solution)/shard_map/ppermute | solution.py:21
  55.7 1.9 collective-permute-start.5
  57.7 1.9 collective-permute-start.6
  59.6 5.1 %collective-permute-start.7 = (f32[8,1,1152]{2,1,0:T(1,128)S(1)}, f32[8,1,1152]{2,1,0:T(1,128)S(1)}, u32[]{:S(2)}, u32[]{:S(2)}) collective-permute-start(f32[8,1,1152]{2,1,0:T(1,128)S(1)} %get-tuple-element.27), channel_id=1, source_target_pairs={{0,32},{32,64},{64,96},{96,128},{128,160},{160,192},{192,224},{224... | collective-permute-start | bytes 110600 | tf_op jit(solution)/shard_map/ppermute | solution.py:20
  64.7 1.8 fusion.52
  66.6 1.4 pad_maximum_fusion.3
  68.0 2.9 %reshape.121 = f32[8,16,24,48]{3,2,1,0:T(8,128)} reshape(f32[8,16,1152]{2,1,0:T(8,128)} %get-tuple-element.20) | data formatting | bytes 1179648 | tf_op jit(solution)/shard_map/reshape | solution.py:58
  70.9 1.8 reshape.122
  72.7 1.8 reshape.123
  74.6 1.8 reshape.124
  76.4 4.8 %fusion.6 = f32[8,16,24,48]{3,2,1,0:T(8,128)S(1)} fusion(f32[7,16,24,48]{3,2,1,0:T(8,128)} %get-tuple-element.19, f32[7,16,24,48]{3,2,1,0:T(8,128)} %get-tuple-element.18, f32[8,16,24,48]{3,2,1,0:T(8,128)} %reshape.124, f32[8,16,24,48]{3,2,1,0:T(8,128)} %reshape.123, f32[8,16,24,48]{3,2,1,0:T(8,128)} %reshape.122, f32[8,16,24,48]{3,2,1,0:T(8,128)} %reshape.121, ...), kind=kLoop, calls=%fused_computation.13 | loop fusion | flops 3244032 | bytes 4608000 | tf_op jit(solution)/shard_map/add | solution.py:36
  82.5 104.5 %all-reduce.4 = (f32[48,48]{1,0:T(8,128)S(1)}, f32[48]{0:T(128)S(1)}) all-reduce(f32[48,48]{1,0:T(8,128)S(1)} %fusion.25, f32[48]{0:T(128)S(1)} %convolution_bitcast_fusion.3), channel_id=1, replica_groups=mesh['lat'=16,'lon'=32] {'lat','lon'}, use_global_device_ids=true, to_apply=%region_1.2 | all-reduce | flops 2352 | bytes 18816 | tf_op jit(solution)/shard_map/psum | solution.py:109
  (75 shorter events, 14.3 us)
Async XLA Ops:
  1.7 25.3 %copy-start.9 = (f32[3,8,16,24]{3,2,1,0:T(8,128)S(1)}, f32[3,8,16,24]{3,2,1,0:T(8,128)}, u32[]{:S(2)}) copy-start(f32[3,8,16,24]{3,2,1,0:T(8,128)} %param.11) | copy-start | bytes 110596
  1.7 25.4 %copy-start.10 = (s32[16,3]{0,1:T(4,128)S(1)}, s32[16,3]{0,1:T(4,128)}, u32[]{:S(2)}) copy-start(s32[16,3]{0,1:T(4,128)} %param.12) | copy-start | bytes 580
  3.3 29.9 %collective-permute-start = (f32[8,16,48]{2,1,0:T(8,128)}, f32[8,16,48]{2,1,0:T(8,128)S(1)}, u32[]{:S(2)}, u32[]{:S(2)}) collective-permute-start(f32[8,16,48]{2,1,0:T(8,128)} %get-tuple-element.32), channel_id=1, source_target_pairs={{1,0},{2,1},{3,2},{4,3},{5,4},{6,5},{7,6},{8,7},{9,8},{10,9},{11,1... | collective-permute-start | bytes 73736 | tf_op jit(solution)/shard_map/ppermute | solution.py:21
  16.2 16.9 %collective-permute-start.1 = (f32[8,16,48]{2,1,0:T(8,128)S(1)}, f32[8,16,48]{2,1,0:T(8,128)S(1)}, u32[]{:S(2)}, u32[]{:S(2)}) collective-permute-start(f32[8,16,48]{2,1,0:T(8,128)S(1)} %get-tuple-element.33), channel_id=1, source_target_pairs={{0,1},{1,2},{2,3},{3,4},{4,5},{5,6},{6,7},{7,8},{8,9},{9,10},{10,1... | collective-permute-start | bytes 73736 | tf_op jit(solution)/shard_map/ppermute | solution.py:20
  18.9 14.3 %collective-permute-start.2 = (f32[8,1,1152]{2,1,0:T(1,128)}, f32[8,1,1152]{2,1,0:T(1,128)}, u32[]{:S(2)}, u32[]{:S(2)}) collective-permute-start(f32[8,1,1152]{2,1,0:T(1,128)} %get-tuple-element.34), channel_id=1, source_target_pairs={{32,0},{64,32},{96,64},{128,96},{160,128},{192,160},{224,192},{256... | collective-permute-start | bytes 110600 | tf_op jit(solution)/shard_map/ppermute | solution.py:21
  21.7 11.4 %collective-permute-start.3 = (f32[8,1,1152]{2,1,0:T(1,128)}, f32[8,1,1152]{2,1,0:T(1,128)}, u32[]{:S(2)}, u32[]{:S(2)}) collective-permute-start(f32[8,1,1152]{2,1,0:T(1,128)} %get-tuple-element.35), channel_id=1, source_target_pairs={{0,32},{32,64},{64,96},{96,128},{128,160},{160,192},{192,224},{224... | collective-permute-start | bytes 110600 | tf_op jit(solution)/shard_map/ppermute | solution.py:20
  27.0 0.9 copy-start.8
  27.0 18.0 %copy-start.2 = (f32[8,16,24]{2,1,0:T(8,128)}, f32[8,16,24]{2,1,0:T(8,128)S(1)}, u32[]{:S(2)}) copy-start(f32[8,16,24]{2,1,0:T(8,128)S(1)} %get-tuple-element.38) | copy-start | bytes 36868
  27.0 18.0 %copy-start.4 = (f32[8,16,24]{2,1,0:T(8,128)}, f32[8,16,24]{2,1,0:T(8,128)S(1)}, u32[]{:S(2)}) copy-start(f32[8,16,24]{2,1,0:T(8,128)S(1)} %get-tuple-element.39) | copy-start | bytes 36868
  27.1 18.0 %copy-start.6 = (f32[8,16,24]{2,1,0:T(8,128)}, f32[8,16,24]{2,1,0:T(8,128)S(1)}, u32[]{:S(2)}) copy-start(f32[8,16,24]{2,1,0:T(8,128)S(1)} %get-tuple-element.40) | copy-start | bytes 36868
  38.4 2.9 %copy-start = (f32[8,16,1152]{2,1,0:T(8,128)S(1)}, f32[8,16,1152]{2,1,0:T(8,128)}, u32[]{:S(2)}) copy-start(f32[8,16,1152]{2,1,0:T(8,128)} %get-tuple-element.30) | copy-start | bytes 1769476
  50.5 16.1 %collective-permute-start.4 = (f32[8,16,48]{2,1,0:T(8,128)S(1)}, f32[8,16,48]{2,1,0:T(8,128)S(1)}, u32[]{:S(2)}, u32[]{:S(2)}) collective-permute-start(f32[8,16,48]{2,1,0:T(8,128)S(1)} %get-tuple-element.24), channel_id=1, source_target_pairs={{1,0},{2,1},{3,2},{4,3},{5,4},{6,5},{7,6},{8,7},{9,8},{10,9},{11,1... | collective-permute-start | bytes 73736 | tf_op jit(solution)/shard_map/ppermute | solution.py:21
  55.7 10.8 %collective-permute-start.5 = (f32[8,16,48]{2,1,0:T(8,128)S(1)}, f32[8,16,48]{2,1,0:T(8,128)S(1)}, u32[]{:S(2)}, u32[]{:S(2)}) collective-permute-start(f32[8,16,48]{2,1,0:T(8,128)S(1)} %get-tuple-element.25), channel_id=1, source_target_pairs={{0,1},{1,2},{2,3},{3,4},{4,5},{5,6},{6,7},{7,8},{8,9},{9,10},{10,1... | collective-permute-start | bytes 73736 | tf_op jit(solution)/shard_map/ppermute | solution.py:20
  57.7 8.9 %collective-permute-start.6 = (f32[8,1,1152]{2,1,0:T(1,128)S(1)}, f32[8,1,1152]{2,1,0:T(1,128)S(1)}, u32[]{:S(2)}, u32[]{:S(2)}) collective-permute-start(f32[8,1,1152]{2,1,0:T(1,128)S(1)} %get-tuple-element.26), channel_id=1, source_target_pairs={{32,0},{64,32},{96,64},{128,96},{160,128},{192,160},{224,192},{256... | collective-permute-start | bytes 110600 | tf_op jit(solution)/shard_map/ppermute | solution.py:21
  59.6 7.0 %collective-permute-start.7 = (f32[8,1,1152]{2,1,0:T(1,128)S(1)}, f32[8,1,1152]{2,1,0:T(1,128)S(1)}, u32[]{:S(2)}, u32[]{:S(2)}) collective-permute-start(f32[8,1,1152]{2,1,0:T(1,128)S(1)} %get-tuple-element.27), channel_id=1, source_target_pairs={{0,32},{32,64},{64,96},{96,128},{128,160},{160,192},{192,224},{224... | collective-permute-start | bytes 110600 | tf_op jit(solution)/shard_map/ppermute | solution.py:20
  68.0 2.9 %copy-start.1 = (f32[8,16,1152]{2,1,0:T(8,128)S(1)}, f32[8,16,1152]{2,1,0:T(8,128)}, u32[]{:S(2)}) copy-start(f32[8,16,1152]{2,1,0:T(8,128)} %get-tuple-element.21) | copy-start | bytes 1769476
  74.5 1.8 copy-start.3
  74.5 1.8 copy-start.5
  74.5 1.8 copy-start.7
  76.4 5.6 %copy-start.11 = (f32[16]{0:T(128)S(1)}, f32[16]{0:T(128)}, u32[]{:S(2)}) copy-start(f32[16]{0:T(128)} %param.15) | copy-start | bytes 196
  76.4 5.9 %copy-start.12 = (f32[16]{0:T(128)S(1)}, f32[16]{0:T(128)}, u32[]{:S(2)}) copy-start(f32[16]{0:T(128)} %param.14) | copy-start | bytes 196
where the time goes:
time: 196 us; the launch traced here: 195 us
  blocking collectives  105 us (54%)
  starting transfers between devices  36.4 us (19%)
  local copies, waits for them, and re-layouts  31.7 us (16%)
  other arithmetic  15.1 us (8%)
  matrix products  4.89 us (2%)
  between operations  2.51 us (1%)
    psum x1, blocking collectives, on_device(): gram, proj = lax.psum((gram_part, proj_part), ('lat', 'lon'))  105 us
    ppermute x4, starting transfers between devices, with_halo(): after = lax.ppermute(leading, axis, down)  23 us
    reshape x9, local copies, waits for them, and re-layouts, as_members(): return flat.reshape(flat.shape[0], flat.shape[1], columns, M)  18.5 us
    ppermute x4, starting transfers between devices, with_halo(): before = lax.ppermute(last, axis, up)  13.4 us
    add x2, other arithmetic, advance(): result - 0.5 * wind_w * (above - below)  9.61 us
    slice x3, local copies, waits for them, and re-layouts, advance(): above = jnp.concatenate([center[1:], zeros], axis=0)  5.45 us
  transfers between devices with their start and end apart: 8, of which 0 were waited for; matrix products, arithmetic and copies ran while one was open for 4% of the time, Pallas kernels for 0%

commit v1 on v0

v1 whole, which is shorter than its diff:
```python
import functools

import jax
import jax.numpy as jnp
from jax import lax
from jax.experimental import pallas as pl
from jax.experimental.pallas import tpu as pltpu
from jax.sharding import PartitionSpec as P

M = 48
NS_ITERS = 5
KH = 0.15
MESH = pl.DeviceIdType.MESH
HP = lax.Precision.HIGHEST
F32 = jnp.float32
BF16 = jnp.bfloat16

LEV, ROWS, COLS, OBS = 8, 16, 24, 16
TILES = 9
WIDTH = COLS * M
WIDE = WIDTH + 256
EAST, WEST = WIDTH, WIDTH + 128
ROWS_X = ROWS + 4
SOUTH, NORTH = ROWS, ROWS + 3
GROUP = 8 * M


def kernel(
    n_lat, n_lon,
    tracer, flux, winds, cells, count, value, var,
    tracer_out, flux_out,
    raw, raw_flux, raw_winds, wide_winds, field, mid, last, wc, wx, wcol_out, wcol_in,
    seen, vals, pack, part1, part2, part3, sum1, sum2, high, low, outs, outs_flux,
    in_sem, out_sem, halo_send, halo_recv, ar_send, ar_recv,
):
    lat, lon = lax.axis_index("lat"), lax.axis_index("lon")

    def at(dlat, dlon):
        return (lax.rem(lat + (dlat + n_lat), n_lat), lax.rem(lon + (dlon + n_lon), n_lon))

    copies = [
        pltpu.make_async_copy(winds, raw_winds, in_sem.at[0]),
    ]
    for t in range(TILES):
        lanes = pl.ds(t * 128, 128)
        copies.append(pltpu.make_async_copy(tracer.at[:, lanes], raw.at[t], in_sem.at[1 + t]))
        copies.append(pltpu.make_async_copy(flux.at[:, lanes], raw_flux.at[t], in_sem.at[1 + TILES + t]))
    for copy in copies:
        copy.start()

    sides = [(1, 0), (-1, 0), (0, 1), (0, -1), (1, 1), (1, -1), (-1, 1), (-1, -1)]
    pair = lax.rem(lon, 2)
    base = lon - pair

    def plane_peer(j):
        return (lax.rem(lat + j // 2, n_lat), base + lax.rem(pair + j, 2))

    def line_peer(j):
        return (lat, lax.rem(lon + 2 * j, n_lon))

    core = lax.rem(lat, 2)
    partner = (lat + 1 - 2 * core, lon)
    n_plane, n_line = 2 * n_lat, n_lon // 2

    barrier = pltpu.get_barrier_semaphore()
    for dlat, dlon in sides:
        pl.semaphore_signal(barrier, inc=1, device_id=at(dlat, dlon), device_id_type=MESH)
    for j in range(1, n_plane):
        pl.semaphore_signal(barrier, inc=1, device_id=plane_peer(j), device_id_type=MESH)
    for j in range(1, n_line):
        pl.semaphore_signal(barrier, inc=1, device_id=line_peer(j), device_id_type=MESH)

    for copy in copies:
        copy.wait()
    level = lax.broadcasted_iota(jnp.int32, (LEV, 1), 0)
    wide_winds[:, 0:COLS] = 0.5 * raw_winds[...]

    def enter(r, carry):
        for t in range(TILES):
            own = raw[t, pl.ds(r, LEV, stride=ROWS), :]
            surface = raw_flux[t, pl.ds(r, 1), :]
            field[r, :, t * 128:t * 128 + 128] = own + jnp.where(level == 0, surface, 0.0)
        for v in range(3):
            wc[v, r] = wide_winds[pl.ds(v * LEV * ROWS + r, LEV, stride=ROWS), :]
        return carry

    lax.fori_loop(0, ROWS, enter, 0)

    lane = lax.broadcasted_iota(jnp.int32, (LEV, 128), 1)

    def edge(r, carry):
        first, final = carry
        for v in range(3):
            w = wc[v, r]
            here = lane == v * ROWS + r
            first = jnp.where(here, w[:, 0:1], first)
            final = jnp.where(here, w[:, COLS - 1:COLS], final)
        return first, final

    zero_tile = jnp.zeros((LEV, 128), F32)
    first, final = lax.fori_loop(0, ROWS, edge, (zero_tile, zero_tile))
    wcol_out[0] = first
    wcol_out[1] = final

    pl.semaphore_wait(barrier, len(sides) + n_plane - 1 + n_line - 1)

    def send(i, src, dst, to):
        return pltpu.make_async_remote_copy(
            src_ref=src, dst_ref=dst, send_sem=halo_send.at[i], recv_sem=halo_recv.at[i],
            device_id=to, device_id_type=MESH,
        )

    own_lanes = pl.ds(0, WIDTH)
    left_tile, right_tile = pl.ds(0, 128), pl.ds(WIDTH - 128, 128)
    east_tile, west_tile = pl.ds(EAST, 128), pl.ds(WEST, 128)
    own_rows = pl.ds(0, ROWS)
    top, bottom = 0, ROWS - 1
    halos = [
        send(0, wcol_out.at[0], wcol_in.at[0], at(0, -1)),
        send(1, wcol_out.at[1], wcol_in.at[1], at(0, 1)),
        send(2, wc.at[:, top], wc.at[:, SOUTH], at(-1, 0)),
        send(3, wc.at[:, bottom], wc.at[:, NORTH], at(1, 0)),
        send(4, field.at[pl.ds(top, 2), :, own_lanes], field.at[pl.ds(SOUTH, 2), :, own_lanes], at(-1, 0)),
        send(5, field.at[pl.ds(bottom - 1, 2), :, own_lanes], field.at[pl.ds(NORTH - 1, 2), :, own_lanes], at(1, 0)),
        send(6, field.at[own_rows, :, left_tile], field.at[own_rows, :, east_tile], at(0, -1)),
        send(7, field.at[own_rows, :, right_tile], field.at[own_rows, :, west_tile], at(0, 1)),
        send(8, field.at[top, :, left_tile], field.at[SOUTH, :, east_tile], at(-1, -1)),
        send(9, field.at[top, :, right_tile], field.at[SOUTH, :, west_tile], at(-1, 1)),
        send(10, field.at[bottom, :, left_tile], field.at[NORTH, :, east_tile], at(1, -1)),
        send(11, field.at[bottom, :, right_tile], field.at[NORTH, :, west_tile], at(1, 1)),
    ]
    for copy in halos[4:] + halos[:4]:
        copy.start()

    spread_col = lax.broadcasted_iota(jnp.int32, (COLS, WIDTH), 0)
    spread_lane = lax.broadcasted_iota(jnp.int32, (COLS, WIDTH), 1)
    spread = jnp.where((spread_lane >= spread_col * M) & (spread_lane < spread_col * M + M), 1.0, 0.0).astype(BF16)

    def spread_rows(v, start, rows):
        w = wc[v, pl.ds(start, rows), :, 0:COLS].reshape(rows * LEV, COLS)
        a = w.astype(BF16)
        rest = w - a.astype(F32)
        b = rest.astype(BF16)
        c = (rest - b.astype(F32)).astype(BF16)
        wide = (
            jnp.dot(a, spread, preferred_element_type=F32)
            + jnp.dot(b, spread, preferred_element_type=F32)
            + jnp.dot(c, spread, preferred_element_type=F32)
        )
        wx[v, pl.ds(start, rows), :, 0:WIDTH] = wide.reshape(rows, LEV, WIDTH)

    for v in range(3):
        spread_rows(v, 0, ROWS)

    for i in range(4):
        halos[i].wait_recv()
    for v in range(3):
        spread_rows(v, SOUTH, 1)
        spread_rows(v, NORTH, 1)
        for side, start in ((0, EAST), (1, WEST)):
            got = wcol_in[side]
            for r in range(ROWS):
                wx[v, r, :, start:start + 128] = jnp.broadcast_to(got[:, v * ROWS + r:v * ROWS + r + 1], (LEV, 128))

    for i in range(4, 12):
        halos[i].wait_recv()

    has_north, has_south = lat > 0, lat < n_lat - 1
    field[NORTH] = jnp.where(has_north, field[NORTH], 0.0)
    field[SOUTH] = jnp.where(has_south, field[SOUTH], 0.0)

    def advance(src, r):
        c = src[r]
        north, south = src[lax.rem(r + ROWS_X - 1, ROWS_X)], src[lax.rem(r + 1, ROWS_X)]
        east, west = pltpu.roll(c, WIDE - M, 1), pltpu.roll(c, M, 1)
        above = jnp.where(level == LEV - 1, 0.0, pltpu.roll(c, LEV - 1, 0))
        below = jnp.where(level == 0, 0.0, pltpu.roll(c, 1, 0))
        spread_out = (east + west) + (south + north) + (above + below)
        carried = wx[0, r] * (east - west) + wx[1, r] * (south - north) + wx[2, r] * (above - below)
        return (1.0 - 6.0 * KH) * c + KH * spread_out - carried

    def first_step(i, carry):
        r = lax.rem(i + NORTH, ROWS_X)
        keep = ((r != NORTH) | has_north) & ((r != SOUTH) | has_south)
        mid[r] = jnp.where(keep, advance(field, r), 0.0)
        return carry

    lax.fori_loop(0, ROWS + 2, first_step, 0)

    def second_step(r, carry):
        new = advance(mid, r)
        for t in range(TILES):
            last[t, pl.ds(pl.multiple_of(r * LEV, LEV), LEV), :] = new[:, t * 128:t * 128 + 128]
        return carry

    lax.fori_loop(0, ROWS, second_step, 0)

    lane_1 = lax.broadcasted_iota(jnp.int32, (1, 128), 1)

    def look(k, carry):
        row, col, lev = cells[0, k] - lat * ROWS, cells[1, k] - lon * COLS, cells[2, k]
        cell = jnp.clip(row * LEV + lev, 0, LEV * ROWS - 1)
        for t in range(TILES):
            line = last[t, pl.ds(cell, 1), :]
            inside = (lane_1 >= col * M - t * 128) & (lane_1 < col * M + M - t * 128)
            seen[t, pl.ds(k, 1), :] = jnp.where(inside, line, 0.0)
        live = jnp.where(k < count[0], 1.0, 0.0)
        vals[0, pl.ds(k, 1), :] = jnp.full((1, 128), live, F32)
        vals[1, pl.ds(k, 1), :] = jnp.full((1, 128), var[k], F32)
        vals[2, pl.ds(k, 1), :] = jnp.full((1, 128), value[k], F32)
        return carry

    lax.fori_loop(0, OBS, look, 0)
    hx = jnp.concatenate([seen[t] + seen[t + 3] + seen[t + 6] for t in range(3)], axis=1)
    hx = hx + pltpu.roll(hx, GROUP // 2, 1)
    hx = hx + pltpu.roll(hx, GROUP // 4, 1)
    hx = hx + pltpu.roll(hx, GROUP // 8, 1)
    lane_o = lax.broadcasted_iota(jnp.int32, (OBS, 128), 1)
    hbar = jnp.sum(jnp.where(lane_o < M, hx[:, 0:128], 0.0), axis=1, keepdims=True) * (1.0 / M)
    y = hx - hbar
    q = vals[0] / vals[1]
    d = vals[2] - hbar

    y0 = y[:, 0:128]
    y32 = pltpu.roll(y, 32, 1)[:, 0:128]
    w0 = jnp.where(lane_o < 48, y0, jnp.where(lane_o == 96, d, 0.0))
    w1 = jnp.where((lane_o >= 48) & (lane_o < 80), y32, jnp.where(lane_o == 97, d, 0.0))
    w2 = jnp.where((lane_o >= 80) & (lane_o < 96), y0, jnp.where(lane_o == 98, d, 0.0))
    l1 = pltpu.roll(y, GROUP - 16, 1)[:, 0:128]
    l2 = pltpu.roll(y, GROUP - 32, 1)[:, 0:128]
    lhs = jnp.concatenate([q * y0, q * l1, q * l2], axis=0)
    rhs = jnp.concatenate([w0, w1, w2], axis=0)
    packed = lax.dot_general(lhs, rhs, (((0,), (0,)), ((), ())), precision=HP, preferred_element_type=F32)[0:16]
    pack[...] = packed.reshape(2, 8, 128)

    for j in range(1, n_plane):
        pltpu.make_async_remote_copy(
            src_ref=pack.at[lax.rem(lat + j // 2, 2)], dst_ref=part1.at[j - 1],
            send_sem=ar_send.at[0], recv_sem=ar_recv.at[0], device_id=plane_peer(j), device_id_type=MESH,
        ).start()

    def halves(x, start, rows):
        for t in range(TILES):
            part = x[t]
            hi = part.astype(BF16)
            place = (pl.ds(t // 3 * 144 + start, rows), pl.ds(t % 3 * 128, 128))
            high[place] = hi
            low[place] = (part - hi.astype(F32)).astype(BF16)

    halves(last, 0, LEV * ROWS)
    halves(raw_flux, LEV * ROWS, ROWS)

    def wait_all(ref, sem):
        pltpu.make_async_copy(ref, ref, sem).wait()

    wait_all(part1, ar_recv.at[0])
    sum1[...] = pack[core] + jnp.sum(part1[...], axis=0)
    for j in range(1, n_line):
        pltpu.make_async_remote_copy(
            src_ref=sum1, dst_ref=part2.at[j - 1],
            send_sem=ar_send.at[1], recv_sem=ar_recv.at[1], device_id=line_peer(j), device_id_type=MESH,
        ).start()
    wait_all(part2, ar_recv.at[1])
    sum2[...] = sum1[...] + jnp.sum(part2[...], axis=0)
    swap = pltpu.make_async_remote_copy(
        src_ref=sum2, dst_ref=part3, send_sem=ar_send.at[2], recv_sem=ar_recv.at[2],
        device_id=partner, device_id_type=MESH,
    )
    swap.start()
    swap.wait_recv()
    mine, other = sum2[...], part3[...]
    total = jnp.concatenate([jnp.where(core == 0, mine, other), jnp.where(core == 0, other, mine)], axis=0)

    lane_p = lax.broadcasted_iota(jnp.int32, (16, 128), 1)
    u0 = jnp.where(lane_p < 48, total, 0.0)
    u1 = jnp.where((lane_p >= 16) & (lane_p < 48), pltpu.roll(total, 128 - 32, 1), 0.0)
    u2 = jnp.where((lane_p >= 32) & (lane_p < 48), pltpu.roll(total, 128 - 48, 1), 0.0)
    upper = jnp.concatenate([u0, u1, u2, jnp.zeros((80, 128), F32)], axis=0)
    flipped = upper.T
    row_s = lax.broadcasted_iota(jnp.int32, (M, M), 0)
    col_s = lax.broadcasted_iota(jnp.int32, (M, M), 1)
    gram = jnp.where(row_s // 16 > col_s // 16, flipped[0:M, 0:M], upper[0:M, 0:M])
    proj = jnp.concatenate([total[:, 96:97], total[:, 97:98], total[:, 98:99]], axis=0)
    eye = jnp.where(row_s == col_s, 1.0, 0.0)

    def dot(a, b):
        return jnp.dot(a, b, precision=HP, preferred_element_type=F32)

    system = (M - 1.0) * eye + gram
    scale = jnp.sqrt(jnp.sum(system * system, keepdims=True))
    root_now = system / scale
    factor = 0.5 * (3.0 * eye - root_now)
    root_now, inverse_now = dot(root_now, factor), factor
    for step in range(1, NS_ITERS):
        factor = 0.5 * (3.0 * eye - dot(inverse_now, root_now))
        if step < NS_ITERS - 1:
            root_now = dot(root_now, factor)
        inverse_now = dot(factor, inverse_now)
    inner = jnp.sum(inverse_now * proj, axis=0, keepdims=True)
    wmean = jnp.sum(inverse_now * inner, axis=1, keepdims=True) / scale
    mixed = wmean + jnp.sqrt((M - 1.0) / scale) * inverse_now
    mixing = mixed - jnp.sum(mixed, axis=0, keepdims=True) * (1.0 / M) + 1.0 / M

    g_high = mixing.astype(BF16)
    g_low = (mixing - g_high.astype(F32)).astype(BF16)
    rep_row = lax.broadcasted_iota(jnp.int32, (M, GROUP), 0)
    rep_lane = lax.broadcasted_iota(jnp.int32, (M, GROUP), 1)
    rep = jnp.where(lax.rem(rep_lane, M) == rep_row, 1.0, 0.0).astype(BF16)
    g_high = jnp.dot(g_high, rep, preferred_element_type=F32)
    g_low = jnp.dot(g_low, rep, preferred_element_type=F32)

    def diagonal(g):
        return jnp.concatenate(
            [jnp.where((rep_lane >= b * M) & (rep_lane < b * M + M), g, 0.0).astype(BF16) for b in range(8)], axis=0
        )

    d_high, d_low = diagonal(g_high), diagonal(g_low)
    for g in range(3):
        hi, lo = high[pl.ds(g * 144, 144), :], low[pl.ds(g * 144, 144), :]
        out = (
            jnp.dot(hi, d_high, preferred_element_type=F32)
            + jnp.dot(lo, d_high, preferred_element_type=F32)
            + jnp.dot(hi, d_low, preferred_element_type=F32)
        )
        lanes = pl.ds(g * GROUP, GROUP)
        for t in range(3):
            for r in range(ROWS):
                outs[g * 3 + t, pl.ds(r, LEV, stride=ROWS), :] = out[r * LEV:(r + 1) * LEV, t * 128:t * 128 + 128]
        outs_flux[:, lanes] = out[LEV * ROWS:]
    done = [
        pltpu.make_async_copy(outs.at[t], tracer_out.at[:, pl.ds(t * 128, 128)], out_sem.at[t]) for t in range(TILES)
    ] + [pltpu.make_async_copy(outs_flux, flux_out, out_sem.at[TILES])]
    for copy in done:
        copy.start()
    for copy in halos:
        copy.wait_send()
    wait_all(part1, ar_send.at[0])
    wait_all(part2, ar_send.at[1])
    swap.wait_send()
    for copy in done:
        copy.wait()


def on_device(n_lat, n_lon, tracer, flux, winds, obs_cells, obs_count, obs_value, obs_var):
    anywhere = pl.BlockSpec(memory_space=pl.ANY)
    scalars = pl.BlockSpec(memory_space=pltpu.SMEM)
    n_plane, n_line = 2 * n_lat, n_lon // 2
    vmem = pltpu.VMEM
    tracer_out, flux_out = pl.pallas_call(
        functools.partial(kernel, n_lat, n_lon),
        out_shape=(
            jax.ShapeDtypeStruct((LEV * ROWS, WIDTH), F32),
            jax.ShapeDtypeStruct((ROWS, WIDTH), F32),
        ),
        in_specs=[anywhere] * 3 + [scalars] * 4,
        out_specs=(anywhere, anywhere),
        scratch_shapes=[
            vmem((TILES, LEV * ROWS, 128), F32),
            vmem((TILES, ROWS, 128), F32),
            vmem((3 * LEV * ROWS, COLS), F32),
            vmem((3 * LEV * ROWS, 128), F32),
            vmem((ROWS_X, LEV, WIDE), F32),
            vmem((ROWS_X, LEV, WIDE), F32),
            vmem((TILES, LEV * ROWS, 128), F32),
            vmem((3, ROWS_X, LEV, 128), F32),
            vmem((3, ROWS_X, LEV, WIDE), F32),
            vmem((2, LEV, 128), F32),
            vmem((2, LEV, 128), F32),
            vmem((TILES, OBS, 128), F32),
            vmem((3, OBS, 128), F32),
            vmem((2, 8, 128), F32),
            vmem((n_plane - 1, 8, 128), F32),
            vmem((n_line - 1, 8, 128), F32),
            vmem((8, 128), F32),
            vmem((8, 128), F32),
            vmem((8, 128), F32),
            vmem((432, GROUP), BF16),
            vmem((432, GROUP), BF16),
            vmem((TILES, LEV * ROWS, 128), F32),
            vmem((ROWS, WIDTH), F32),
            pltpu.SemaphoreType.DMA((1 + 2 * TILES,)),
            pltpu.SemaphoreType.DMA((1 + TILES,)),
            pltpu.SemaphoreType.DMA((12,)),
            pltpu.SemaphoreType.DMA((12,)),
            pltpu.SemaphoreType.DMA((3,)),
            pltpu.SemaphoreType.DMA((3,)),
        ],
        compiler_params=pltpu.CompilerParams(
            collective_id=0, has_side_effects=True, vmem_limit_bytes=48 * 1024 * 1024
        ),
        name="analysis",
    )(
        tracer.reshape(LEV * ROWS, WIDTH), flux, winds.reshape(3 * LEV * ROWS, COLS),
        obs_cells.T, obs_count, obs_value, obs_var,
    )
    return tracer_out.reshape(LEV, ROWS, WIDTH), flux_out


def solution(mesh):
    return jax.shard_map(
        functools.partial(on_device, mesh.shape["lat"], mesh.shape["lon"]),
        mesh=mesh,
        in_specs=(
            P(None, "lat", "lon"),
            P("lat", "lon"),
            P(None, None, "lat", "lon"),
            P(("lat", "lon"), None),
            P(("lat", "lon")),
            P(("lat", "lon")),
            P(("lat", "lon")),
        ),
        out_specs=(P(None, "lat", "lon"), P("lat", "lon")),
        check_vma=False,
    )
```

time: 196 us -> 54.3 us (0.28)
  blocking collectives: 105 us -> 0 us
  Pallas kernels: 0 us -> 47.7 us
  starting transfers between devices: 36.4 us -> 0 us
  local copies, waits for them, and re-layouts: 31.7 us -> 4.99 us
  other arithmetic: 15.1 us -> 0 us
  matrix products: 4.89 us -> 0 us
    psum x1 -> x0, blocking collectives: 105 us -> none  [on_device(): gram, proj = lax.psum((gram_part, proj_part), ('lat', 'lon'))]
    pallas_call x0 -> x1, Pallas kernels: none -> 47.7 us  [on_device(): pl.pallas_call(functools.partial(kernel, n_lat, n_lon), out_shape=(jax.Sh...]
    ppermute x8 -> x0, starting transfers between devices: 36.4 us -> none  [the longest x4 23 us: with_halo(): after = lax.ppermute(leading, axis, down)]
    reshape x13 -> x0, local copies, waits for them, and re-layouts: 21.2 us -> none  [the longest x9 18.5 us: as_members(): return flat.reshape(flat.shape[0], flat.shape[1], columns, M)]
    add x2 -> x0, other arithmetic: 9.61 us -> none  [advance(): result - 0.5 * wind_w * (above - below)]
    slice x8 -> x0, local copies, waits for them, and re-layouts: 8.57 us -> none  [the longest x3 5.45 us: advance(): above = jnp.concatenate([center[1:], zeros], axis=0)]
    dot_general x21 -> x0, matrix products: 4.89 us -> none  [the longest x1 1.38 us: on_device(): jnp.dot(member_rows, mixing, precision=hp).reshape(levels, rows, width)]
    concatenate x2 -> x0, other arithmetic: 3.76 us -> none  [with_halo(): value = jnp.concatenate([before, value, after], axis=dim)]
  transfers between devices with their start and end apart: 8 -> 0, of which waited for: 0 -> 0; matrix products, arithmetic and copies ran while one was open for 4% -> 0% of each run, Pallas kernels for 0% -> 0%
where the time goes in v1:
time: 54.3 us; the launch traced here: 54 us
  Pallas kernels  47.7 us (88%)
  local copies, waits for them, and re-layouts  4.99 us (9%)
  between operations  1.31 us (2%)
    pallas_call x1, Pallas kernels, on_device(): pl.pallas_call(functools.partial(kernel, n_lat, n_lon), out_shape=(jax.Sh...  47.7 us
    unnamed x14, local copies, waits for them, and re-layouts  4.99 us

profile of v1, /device:TPU:1, one launch (start us, length us, event | category | flops | bytes accessed | tf_op | source)
XLA Modules:
  0.0 54.0 jit_solution(11261396121033663036)
XLA Ops:
  1.3 0.0 copy-start.3
  1.3 0.0 copy-start.4
  1.3 0.0 copy-start.5
  1.3 0.7 %copy-done.3 = s32[16,3]{0,1:T(4,128)S(1)} copy-done((s32[16,3]{0,1:T(4,128)S(1)}, s32[16,3]{0,1:T(4,128)}, u32[]{:S(2)}) %copy-start.3) | copy-done | bytes 216
  2.0 0.0 copy-done.4
  2.0 0.0 copy-done.5
  2.0 0.0 copy-start
  2.0 1.1 %copy-done = f32[8,16,1152]{2,1,0:T(8,128)S(1)} copy-done((f32[8,16,1152]{2,1,0:T(8,128)S(1)}, f32[8,16,1152]{2,1,0:T(8,128)}, u32[]{:S(2)}) %copy-start) | copy-done | bytes 589848
  3.0 0.0 copy-start.1
  3.0 0.9 %copy-done.1 = f32[3,8,16,24]{3,2,1,0:T(8,128)S(1)} copy-done((f32[3,8,16,24]{3,2,1,0:T(8,128)S(1)}, f32[3,8,16,24]{3,2,1,0:T(8,128)}, u32[]{:S(2)}) %copy-start.1) | copy-done | bytes 36888
  4.0 0.0 copy-start.2
  4.0 0.9 %copy-done.2 = f32[16,1152]{1,0:T(8,128)S(1)} copy-done((f32[16,1152]{1,0:T(8,128)S(1)}, f32[16,1152]{1,0:T(8,128)}, u32[]{:S(2)}) %copy-start.2) | copy-done | bytes 73752
  4.8 47.7 %analysis.1 = (f32[128,1152]{1,0:T(8,128)S(1)}, f32[16,1152]{1,0:T(8,128)S(1)}) custom-call(f32[128,1152]{1,0:T(8,128)S(1)} %bitcast.4, f32[16,1152]{1,0:T(8,128)S(1)} %copy-done.2, f32[384,24]{1,0:T(8,128)S(1)} %bitcast.6, s32[3,16]{1,0:T(4,128)S(1)} %bitcast.7, s32[1]{0:T(128)S(6)} %copy.11.count, f32[16]{0:T(128)S(1)} %copy-done.4, f32[16]{0:T(128)S(1)} %copy-done.5), custom_call_target="tpu_custom_call" | custom-call | tf_op jit(solution)/shard_map/analysis/pallas_call | solution.py:349
  52.6 0.8 %copy.12 = f32[8,16,1152]{2,1,0:T(8,128)} copy(f32[8,16,1152]{2,1,0:T(8,128)S(1)} %bitcast.5) | data formatting | bytes 1179648
  53.4 0.6 %copy.13 = f32[16,1152]{1,0:T(8,128)} copy(f32[16,1152]{1,0:T(8,128)S(1)} %get-tuple-element.9) | data formatting | bytes 147456
Async XLA Ops:
  1.3 0.7 %copy-start.3 = (s32[16,3]{0,1:T(4,128)S(1)}, s32[16,3]{0,1:T(4,128)}, u32[]{:S(2)}) copy-start(s32[16,3]{0,1:T(4,128)} %param.10) | copy-start | bytes 580
  1.3 0.7 %copy-start.4 = (f32[16]{0:T(128)S(1)}, f32[16]{0:T(128)}, u32[]{:S(2)}) copy-start(f32[16]{0:T(128)} %value.1) | copy-start | bytes 196
  1.3 0.7 %copy-start.5 = (f32[16]{0:T(128)S(1)}, f32[16]{0:T(128)}, u32[]{:S(2)}) copy-start(f32[16]{0:T(128)} %var.1) | copy-start | bytes 196
  2.0 1.1 %copy-start = (f32[8,16,1152]{2,1,0:T(8,128)S(1)}, f32[8,16,1152]{2,1,0:T(8,128)}, u32[]{:S(2)}) copy-start(f32[8,16,1152]{2,1,0:T(8,128)} %param.7) | copy-start | bytes 1769476
  3.0 0.9 %copy-start.1 = (f32[3,8,16,24]{3,2,1,0:T(8,128)S(1)}, f32[3,8,16,24]{3,2,1,0:T(8,128)}, u32[]{:S(2)}) copy-start(f32[3,8,16,24]{3,2,1,0:T(8,128)} %param.9) | copy-start | bytes 110596
  4.0 0.9 %copy-start.2 = (f32[16,1152]{1,0:T(8,128)S(1)}, f32[16,1152]{1,0:T(8,128)}, u32[]{:S(2)}) copy-start(f32[16,1152]{1,0:T(8,128)} %flux.1) | copy-start | bytes 221188

commit v2 on v1

--- a/solution.py
+++ b/solution.py
@@ -27,11 +27,11 @@
 
 def kernel(
     n_lat, n_lon,
-    tracer, flux, winds, cells, count, value, var,
+    tracer, flux, winds, cells_in, count_in, value_in, var_in,
     tracer_out, flux_out,
     raw, raw_flux, raw_winds, wide_winds, field, mid, last, wc, wx, wcol_out, wcol_in,
-    seen, vals, pack, part1, part2, part3, sum1, sum2, high, low, outs, outs_flux,
-    in_sem, out_sem, halo_send, halo_recv, ar_send, ar_recv,
+    seen, vals, pack, part1, part2, part3, sum1, sum2, high, low,
+    cells, count, value, var, in_sem, halo_send, halo_recv, ar_send, ar_recv, here_sem,
 ):
     lat, lon = lax.axis_index("lat"), lax.axis_index("lon")
 
@@ -45,7 +45,11 @@
         lanes = pl.ds(t * 128, 128)
         copies.append(pltpu.make_async_copy(tracer.at[:, lanes], raw.at[t], in_sem.at[1 + t]))
         copies.append(pltpu.make_async_copy(flux.at[:, lanes], raw_flux.at[t], in_sem.at[1 + TILES + t]))
-    for copy in copies:
+    obs_copies = [
+        pltpu.make_async_copy(src, dst, in_sem.at[1 + 2 * TILES + i])
+        for i, (src, dst) in enumerate(((cells_in, cells), (count_in, count), (value_in, value), (var_in, var)))
+    ]
+    for copy in copies + obs_copies:
         copy.start()
 
     sides = [(1, 0), (-1, 0), (0, 1), (0, -1), (1, 1), (1, -1), (-1, 1), (-1, -1)]
@@ -62,13 +66,16 @@
     partner = (lat + 1 - 2 * core, lon)
     n_plane, n_line = 2 * n_lat, n_lon // 2
 
+    near = [k for k in (4, -4, 3, -3, 1, -1)]
+    plane_order = sorted(range(1, n_plane), key=lambda j: -min(j // 2, n_lat - j // 2))
+    line_order = sorted(range(1, n_line), key=lambda j: -min(j, n_line - j))
     barrier = pltpu.get_barrier_semaphore()
+    for j in plane_order:
+        pl.semaphore_signal(barrier, inc=1, device_id=plane_peer(j), device_id_type=MESH)
     for dlat, dlon in sides:
         pl.semaphore_signal(barrier, inc=1, device_id=at(dlat, dlon), device_id_type=MESH)
-    for j in range(1, n_plane):
-        pl.semaphore_signal(barrier, inc=1, device_id=plane_peer(j), device_id_type=MESH)
-    for j in range(1, n_line):
-        pl.semaphore_signal(barrier, inc=1, device_id=line_peer(j), device_id_type=MESH)
+    for k in near:
+        pl.semaphore_signal(barrier, inc=1, device_id=line_peer(k % n_line), device_id_type=MESH)
 
     for copy in copies:
         copy.wait()
@@ -102,7 +109,7 @@
     wcol_out[0] = first
     wcol_out[1] = final
 
-    pl.semaphore_wait(barrier, len(sides) + n_plane - 1 + n_line - 1)
+    pl.semaphore_wait(barrier, len(sides) + n_plane - 1 + len(near))
 
     def send(i, src, dst, to):
         return pltpu.make_async_remote_copy(
@@ -131,6 +138,8 @@
     ]
     for copy in halos[4:] + halos[:4]:
         copy.start()
+    for k in near:
+        pl.semaphore_signal(here_sem, inc=1, device_id=line_peer(k % n_line), device_id_type=MESH)
 
     spread_col = lax.broadcasted_iota(jnp.int32, (COLS, WIDTH), 0)
     spread_lane = lax.broadcasted_iota(jnp.int32, (COLS, WIDTH), 1)
@@ -152,48 +161,107 @@
     for v in range(3):
         spread_rows(v, 0, ROWS)
 
-    for i in range(4):
+    def stencil(c, n, s, u, v, w, first, final):
+        width = c.shape[1]
+        keep = slice(first, final)
+        east, west = pltpu.roll(c, width - M, 1)[:, keep], pltpu.roll(c, M, 1)[:, keep]
+        c = c[:, keep]
+        above = jnp.where(level == LEV - 1, 0.0, pltpu.roll(c, LEV - 1, 0))
+        below = jnp.where(level == 0, 0.0, pltpu.roll(c, 1, 0))
+        spread_out = (east + west) + (s + n) + (above + below)
+        carried = u * (east - west) + v * (s - n) + w * (above - below)
+        return (1.0 - 6.0 * KH) * c + KH * spread_out - carried
+
+    def strip(src, r, width):
+        n, s = lax.rem(r + ROWS_X - 1, ROWS_X), lax.rem(r + 1, ROWS_X)
+        return stencil(
+            src[r, :, 0:width], src[n, :, 0:width], src[s, :, 0:width],
+            wx[0, r, :, 0:width], wx[1, r, :, 0:width], wx[2, r, :, 0:width], 0, width,
+        )
+
+    def west_end(src, r, first):
+        def of(ref, i):
+            return jnp.concatenate([ref[i, :, WEST:WEST + 128], ref[i, :, 0:128]], axis=1)[:, first:]
+
+        c = jnp.concatenate([src[r, :, WEST:WEST + 128], src[r, :, 0:256]], axis=1)
+        return stencil(
+            c, of(src, r - 1), of(src, r + 1), of(wx.at[0], r), of(wx.at[1], r), of(wx.at[2], r), first, 256
+        )
+
+    def east_end(src, r, final):
+        lanes = slice(WIDTH - 128, WIDTH - 256 + final)
+        return stencil(
+            src[r, :, WIDTH - 256:WIDTH + 128], src[r - 1, :, lanes], src[r + 1, :, lanes],
+            wx[0, r, :, lanes], wx[1, r, :, lanes], wx[2, r, :, lanes], 128, final,
+        )
+
+    def put(r, tiles, value):
+        for i, t in enumerate(tiles):
+            last[t, pl.ds(pl.multiple_of(r * LEV, LEV), LEV), :] = value[:, i * 128:i * 128 + 128]
+
+    def inner_first(r, carry):
+        mid[r, :, 0:WIDTH] = strip(field, r, WIDTH)
+        return carry
+
+    lax.fori_loop(1, ROWS - 1, inner_first, 0, unroll=2)
+
+    def inner_second(r, carry):
+        put(r, range(1, TILES - 1), strip(mid, r, WIDTH)[:, 128:WIDTH - 128])
+        return carry
+
+    lax.fori_loop(2, ROWS - 2, inner_second, 0, unroll=2)
+
+    for copy in obs_copies:
+        copy.wait()
+
+    def note(k, carry):
+        live = jnp.where(k < count[0], 1.0, 0.0)
+        vals[0, pl.ds(k, 1), :] = jnp.full((1, 128), live, F32)
+        vals[1, pl.ds(k, 1), :] = jnp.full((1, 128), var[k], F32)
+        vals[2, pl.ds(k, 1), :] = jnp.full((1, 128), value[k], F32)
+        return carry
+
+    lax.fori_loop(0, OBS, note, 0)
+
+    for i in (0, 1, 6, 7):
+        halos[i].wait_recv()
+    for v in range(3):
+        for side, start in ((0, EAST), (1, WEST)):
+            got = wcol_in[side]
+            for r in range(ROWS):
+                wx[v, r, :, start:start + 128] = jnp.broadcast_to(got[:, v * ROWS + r:v * ROWS + r + 1], (LEV, 128))
+
+    def ends_first(r, carry):
+        new = west_end(field, r, 0)
+        mid[r, :, WEST:WEST + 128] = new[:, 0:128]
+        mid[r, :, 0:128] = new[:, 128:256]
+        mid[r, :, WIDTH - 128:WIDTH + 128] = east_end(field, r, 384)
+        return carry
+
+    lax.fori_loop(1, ROWS - 1, ends_first, 0, unroll=2)
+
+    for i in (2, 3, 4, 5, 8, 9, 10, 11):
         halos[i].wait_recv()
     for v in range(3):
         spread_rows(v, SOUTH, 1)
         spread_rows(v, NORTH, 1)
-        for side, start in ((0, EAST), (1, WEST)):
-            got = wcol_in[side]
-            for r in range(ROWS):
-                wx[v, r, :, start:start + 128] = jnp.broadcast_to(got[:, v * ROWS + r:v * ROWS + r + 1], (LEV, 128))
-
-    for i in range(4, 12):
-        halos[i].wait_recv()
-
     has_north, has_south = lat > 0, lat < n_lat - 1
     field[NORTH] = jnp.where(has_north, field[NORTH], 0.0)
     field[SOUTH] = jnp.where(has_south, field[SOUTH], 0.0)
-
-    def advance(src, r):
-        c = src[r]
-        north, south = src[lax.rem(r + ROWS_X - 1, ROWS_X)], src[lax.rem(r + 1, ROWS_X)]
-        east, west = pltpu.roll(c, WIDE - M, 1), pltpu.roll(c, M, 1)
-        above = jnp.where(level == LEV - 1, 0.0, pltpu.roll(c, LEV - 1, 0))
-        below = jnp.where(level == 0, 0.0, pltpu.roll(c, 1, 0))
-        spread_out = (east + west) + (south + north) + (above + below)
-        carried = wx[0, r] * (east - west) + wx[1, r] * (south - north) + wx[2, r] * (above - below)
-        return (1.0 - 6.0 * KH) * c + KH * spread_out - carried
-
-    def first_step(i, carry):
-        r = lax.rem(i + NORTH, ROWS_X)
-        keep = ((r != NORTH) | has_north) & ((r != SOUTH) | has_south)
-        mid[r] = jnp.where(keep, advance(field, r), 0.0)
-        return carry
-
-    lax.fori_loop(0, ROWS + 2, first_step, 0)
-
-    def second_step(r, carry):
-        new = advance(mid, r)
-        for t in range(TILES):
-            last[t, pl.ds(pl.multiple_of(r * LEV, LEV), LEV), :] = new[:, t * 128:t * 128 + 128]
-        return carry
-
-    lax.fori_loop(0, ROWS, second_step, 0)
+    mid[0] = strip(field, 0, WIDE)
+    mid[ROWS - 1] = strip(field, ROWS - 1, WIDE)
+    mid[NORTH] = jnp.where(has_north, strip(field, NORTH, WIDE), 0.0)
+    mid[SOUTH] = jnp.where(has_south, strip(field, SOUTH, WIDE), 0.0)
+
+    for r in (0, 1, ROWS - 2, ROWS - 1):
+        put(r, range(TILES), strip(mid, r, WIDE)[:, 0:WIDTH])
+
+    def ends_second(r, carry):
+        put(r, (0,), west_end(mid, r, 128))
+        put(r, (TILES - 1,), east_end(mid, r, 256))
+        return carry
+
+    lax.fori_loop(2, ROWS - 2, ends_second, 0, unroll=2)
 
     lane_1 = lax.broadcasted_iota(jnp.int32, (1, 128), 1)
 
@@ -204,13 +272,9 @@
             line = last[t, pl.ds(cell, 1), :]
             inside = (lane_1 >= col * M - t * 128) & (lane_1 < col * M + M - t * 128)
             seen[t, pl.ds(k, 1), :] = jnp.where(inside, line, 0.0)
-        live = jnp.where(k < count[0], 1.0, 0.0)
-        vals[0, pl.ds(k, 1), :] = jnp.full((1, 128), live, F32)
-        vals[1, pl.ds(k, 1), :] = jnp.full((1, 128), var[k], F32)
-        vals[2, pl.ds(k, 1), :] = jnp.full((1, 128), value[k], F32)
-        return carry
-
-    lax.fori_loop(0, OBS, look, 0)
+        return carry
+
+    lax.fori_loop(0, OBS, look, 0, unroll=4)
     hx = jnp.concatenate([seen[t] + seen[t + 3] + seen[t + 6] for t in range(3)], axis=1)
     hx = hx + pltpu.roll(hx, GROUP // 2, 1)
     hx = hx + pltpu.roll(hx, GROUP // 4, 1)
@@ -233,29 +297,28 @@
     packed = lax.dot_general(lhs, rhs, (((0,), (0,)), ((), ())), precision=HP, preferred_element_type=F32)[0:16]
     pack[...] = packed.reshape(2, 8, 128)
 
-    for j in range(1, n_plane):
+    for j in plane_order:
         pltpu.make_async_remote_copy(
             src_ref=pack.at[lax.rem(lat + j // 2, 2)], dst_ref=part1.at[j - 1],
             send_sem=ar_send.at[0], recv_sem=ar_recv.at[0], device_id=plane_peer(j), device_id_type=MESH,
         ).start()
 
-    def halves(x, start, rows):
-        for t in range(TILES):
-            part = x[t]
+    for t in range(TILES):
+        lanes = pl.ds(t % 3 * 128, 128)
+        for lev in range(LEV + 1):
+            part = last[t, pl.ds(lev, ROWS, stride=LEV), :] if lev < LEV else raw_flux[t]
             hi = part.astype(BF16)
-            place = (pl.ds(t // 3 * 144 + start, rows), pl.ds(t % 3 * 128, 128))
-            high[place] = hi
-            low[place] = (part - hi.astype(F32)).astype(BF16)
-
-    halves(last, 0, LEV * ROWS)
-    halves(raw_flux, LEV * ROWS, ROWS)
+            rows = pl.ds(t // 3 * 144 + lev * ROWS, ROWS)
+            high[rows, lanes] = hi
+            low[rows, lanes] = (part - hi.astype(F32)).astype(BF16)
 
     def wait_all(ref, sem):
         pltpu.make_async_copy(ref, ref, sem).wait()
 
     wait_all(part1, ar_recv.at[0])
     sum1[...] = pack[core] + jnp.sum(part1[...], axis=0)
-    for j in range(1, n_line):
+    pl.semaphore_wait(here_sem, len(near))
+    for j in line_order:
         pltpu.make_async_remote_copy(
             src_ref=sum1, dst_ref=part2.at[j - 1],
             send_sem=ar_send.at[1], recv_sem=ar_recv.at[1], device_id=line_peer(j), device_id_type=MESH,
@@ -323,27 +386,17 @@
             + jnp.dot(hi, d_low, preferred_element_type=F32)
         )
         lanes = pl.ds(g * GROUP, GROUP)
-        for t in range(3):
-            for r in range(ROWS):
-                outs[g * 3 + t, pl.ds(r, LEV, stride=ROWS), :] = out[r * LEV:(r + 1) * LEV, t * 128:t * 128 + 128]
-        outs_flux[:, lanes] = out[LEV * ROWS:]
-    done = [
-        pltpu.make_async_copy(outs.at[t], tracer_out.at[:, pl.ds(t * 128, 128)], out_sem.at[t]) for t in range(TILES)
-    ] + [pltpu.make_async_copy(outs_flux, flux_out, out_sem.at[TILES])]
-    for copy in done:
-        copy.start()
+        tracer_out[:, lanes] = out[0:LEV * ROWS]
+        flux_out[:, lanes] = out[LEV * ROWS:]
     for copy in halos:
         copy.wait_send()
     wait_all(part1, ar_send.at[0])
     wait_all(part2, ar_send.at[1])
     swap.wait_send()
-    for copy in done:
-        copy.wait()
 
 
 def on_device(n_lat, n_lon, tracer, flux, winds, obs_cells, obs_count, obs_value, obs_var):
-    anywhere = pl.BlockSpec(memory_space=pl.ANY)
-    scalars = pl.BlockSpec(memory_space=pltpu.SMEM)
+    hbm, local = pl.BlockSpec(memory_space=pltpu.HBM), pl.BlockSpec(memory_space=pltpu.VMEM)
     n_plane, n_line = 2 * n_lat, n_lon // 2
     vmem = pltpu.VMEM
     tracer_out, flux_out = pl.pallas_call(
@@ -352,8 +405,8 @@
             jax.ShapeDtypeStruct((LEV * ROWS, WIDTH), F32),
             jax.ShapeDtypeStruct((ROWS, WIDTH), F32),
         ),
-        in_specs=[anywhere] * 3 + [scalars] * 4,
-        out_specs=(anywhere, anywhere),
+        in_specs=[hbm] * 7,
+        out_specs=(local, local),
         scratch_shapes=[
             vmem((TILES, LEV * ROWS, 128), F32),
             vmem((TILES, ROWS, 128), F32),
@@ -376,17 +429,19 @@
             vmem((8, 128), F32),
             vmem((432, GROUP), BF16),
             vmem((432, GROUP), BF16),
-            vmem((TILES, LEV * ROWS, 128), F32),
-            vmem((ROWS, WIDTH), F32),
-            pltpu.SemaphoreType.DMA((1 + 2 * TILES,)),
-            pltpu.SemaphoreType.DMA((1 + TILES,)),
+            pltpu.SMEM((3, OBS), jnp.int32),
+            pltpu.SMEM((1,), jnp.int32),
+            pltpu.SMEM((OBS,), F32),
+            pltpu.SMEM((OBS,), F32),
+            pltpu.SemaphoreType.DMA((5 + 2 * TILES,)),
             pltpu.SemaphoreType.DMA((12,)),
             pltpu.SemaphoreType.DMA((12,)),
             pltpu.SemaphoreType.DMA((3,)),
             pltpu.SemaphoreType.DMA((3,)),
+            pltpu.SemaphoreType.REGULAR,
         ],
         compiler_params=pltpu.CompilerParams(
-            collective_id=0, has_side_effects=True, vmem_limit_bytes=48 * 1024 * 1024
+            collective_id=0, has_side_effects=True, vmem_limit_bytes=62 * 1024 * 1024
         ),
         name="analysis",
     )(

time: 54.3 us -> 46.8 us (0.86)
  Pallas kernels: 47.7 us -> 42.8 us
  local copies, waits for them, and re-layouts: 4.99 us -> 2.59 us
    pallas_call x1, Pallas kernels: 47.7 us -> 42.8 us  [on_device(): pl.pallas_call(functools.partial(kernel, n_lat, n_lon), out_shape=(jax.Sh...]
    unnamed x14 -> x4, local copies, waits for them, and re-layouts: 4.99 us -> 2.59 us
where the time goes in v2:
time: 46.8 us; the launch traced here: 46.6 us
  Pallas kernels  42.8 us (91%)
  local copies, waits for them, and re-layouts  2.59 us (6%)
  between operations  1.29 us (3%)
    pallas_call x1, Pallas kernels, on_device(): pl.pallas_call(functools.partial(kernel, n_lat, n_lon), out_shape=(jax.Sh...  42.8 us
    unnamed x4, local copies, waits for them, and re-layouts  2.59 us

profile of v2, /device:TPU:1, one launch (start us, length us, event | category | flops | bytes accessed | tf_op | source)
XLA Modules:
  0.0 46.6 jit_solution(5568108031824302798)
XLA Ops:
  1.3 42.8 %analysis.1 = (f32[128,1152]{1,0:T(8,128)}, f32[16,1152]{1,0:T(8,128)}) custom-call(f32[128,1152]{1,0:T(8,128)} %bitcast.4, f32[16,1152]{1,0:T(8,128)} %flux.1, f32[384,24]{1,0:T(8,128)} %bitcast.6, s32[3,16]{1,0:T(4,128)} %bitcast.7, s32[1]{0:T(128)S(6)} %copy.11.count_in, f32[16]{0:T(128)} %value_in.1, f32[16]{0:T(128)} %var_in.1), custom_call_target="tpu_custom_call" | custom-call | tf_op jit(solution)/shard_map/analysis/pallas_call | solution.py:402
  44.0 0.0 copy-start
  44.1 1.9 %copy.12 = f32[8,16,1152]{2,1,0:T(8,128)} copy(f32[8,16,1152]{2,1,0:T(8,128)} %bitcast.5) | data formatting | bytes 1179648
  46.0 0.0 copy-done
  46.0 0.6 %copy.13 = f32[16,1152]{1,0:T(8,128)} copy(f32[16,1152]{1,0:T(8,128)S(1)} %copy-done) | data formatting | bytes 147456
Async XLA Ops:
  44.0 2.0 %copy-start = (f32[16,1152]{1,0:T(8,128)S(1)}, f32[16,1152]{1,0:T(8,128)}, u32[]{:S(2)}) copy-start(f32[16,1152]{1,0:T(8,128)} %get-tuple-element.9) | copy-start | bytes 221188

commit v3 on v2

--- a/solution.py
+++ b/solution.py
@@ -30,13 +30,45 @@
     tracer, flux, winds, cells_in, count_in, value_in, var_in,
     tracer_out, flux_out,
     raw, raw_flux, raw_winds, wide_winds, field, mid, last, wc, wx, wcol_out, wcol_in,
-    seen, vals, pack, part1, part2, part3, sum1, sum2, high, low,
-    cells, count, value, var, in_sem, halo_send, halo_recv, ar_send, ar_recv, here_sem,
+    wrow_out, wrow_in, lon_out, lon_in, seen, vals, pack, part1, part2, part3, sum1, sum2, high, low, outs,
+    cells, count, value, var, in_sem, out_sem, halo_send, halo_recv, ar_send, ar_recv, here_sem,
 ):
     lat, lon = lax.axis_index("lat"), lax.axis_index("lon")
 
     def at(dlat, dlon):
         return (lax.rem(lat + (dlat + n_lat), n_lat), lax.rem(lon + (dlon + n_lon), n_lon))
+
+    sides = [(1, 0), (-1, 0), (0, 1), (0, -1), (1, 1), (1, -1), (-1, 1), (-1, -1)]
+    pair = lax.rem(lon, 2)
+    base = lon - pair
+
+    def plane_peer(j):
+        return (lax.rem(lat + j // 2, n_lat), base + lax.rem(pair + j, 2))
+
+    def line_peer(j):
+        return (lat, lax.rem(lon + 2 * j, n_lon))
+
+    core = lax.rem(lat, 2)
+    partner = (lat + 1 - 2 * core, lon)
+    n_plane, n_line = 2 * n_lat, n_lon // 2
+
+    n_x = n_lat // 4
+    x, y = lat // 4, lax.rem(lat // 2, 2) * 2 + pair
+
+    def plane_near(dx, dy, dc):
+        to_x, to_y = lax.rem(x + (dx + n_x), n_x), lax.rem(y + (dy + 4), 4)
+        return (to_x * 4 + to_y // 2 * 2 + lax.rem(core + dc, 2), base + lax.rem(to_y, 2))
+
+    near_plane = [
+        plane_near(dx, dy, dc) for dx in (-1, 1, 0) for dy in (-1, 1, 0) for dc in (1, 0) if (dx, dy, dc) != (0, 0, 0)
+    ]
+    near_line = [line_peer(k % n_line) for k in (3, -3, 2, -2)]
+    near_halo = [at(dlat, dlon) for dlat, dlon in sides]
+    plane_order = sorted(range(1, n_plane), key=lambda j: -min(j // 2, n_lat - j // 2))
+    line_order = sorted(range(1, n_line), key=lambda j: -min(j, n_line - j))
+    barrier = pltpu.get_barrier_semaphore()
+    for peer in near_halo + near_line + near_plane:
+        pl.semaphore_signal(barrier, inc=1, device_id=peer, device_id_type=MESH)
 
     copies = [
         pltpu.make_async_copy(winds, raw_winds, in_sem.at[0]),
@@ -52,31 +84,6 @@
     for copy in copies + obs_copies:
         copy.start()
 
-    sides = [(1, 0), (-1, 0), (0, 1), (0, -1), (1, 1), (1, -1), (-1, 1), (-1, -1)]
-    pair = lax.rem(lon, 2)
-    base = lon - pair
-
-    def plane_peer(j):
-        return (lax.rem(lat + j // 2, n_lat), base + lax.rem(pair + j, 2))
-
-    def line_peer(j):
-        return (lat, lax.rem(lon + 2 * j, n_lon))
-
-    core = lax.rem(lat, 2)
-    partner = (lat + 1 - 2 * core, lon)
-    n_plane, n_line = 2 * n_lat, n_lon // 2
-
-    near = [k for k in (4, -4, 3, -3, 1, -1)]
-    plane_order = sorted(range(1, n_plane), key=lambda j: -min(j // 2, n_lat - j // 2))
-    line_order = sorted(range(1, n_line), key=lambda j: -min(j, n_line - j))
-    barrier = pltpu.get_barrier_semaphore()
-    for j in plane_order:
-        pl.semaphore_signal(barrier, inc=1, device_id=plane_peer(j), device_id_type=MESH)
-    for dlat, dlon in sides:
-        pl.semaphore_signal(barrier, inc=1, device_id=at(dlat, dlon), device_id_type=MESH)
-    for k in near:
-        pl.semaphore_signal(barrier, inc=1, device_id=line_peer(k % n_line), device_id_type=MESH)
-
     for copy in copies:
         copy.wait()
     level = lax.broadcasted_iota(jnp.int32, (LEV, 1), 0)
@@ -108,8 +115,26 @@
     first, final = lax.fori_loop(0, ROWS, edge, (zero_tile, zero_tile))
     wcol_out[0] = first
     wcol_out[1] = final
-
-    pl.semaphore_wait(barrier, len(sides) + n_plane - 1 + len(near))
+    for side, r in ((0, 0), (1, ROWS - 1)):
+        packed_row = jnp.where(lane < COLS, wc[0, r], 0.0)
+        for v in (1, 2):
+            here = (lane >= v * COLS) & (lane < v * COLS + COLS)
+            packed_row = jnp.where(here, pltpu.roll(wc[v, r], v * COLS, 1), packed_row)
+        wrow_out[side] = packed_row
+
+    def tuck(i, carry):
+        for side, start, free, gap in ((0, 0, 0, 2 * M), (1, WIDTH - 128, 32, 0)):
+            fourth = field[4 * i + 3, :, start:start + 128]
+            for j in range(3):
+                shift = (gap - free - 32 * j) % 128
+                moved = pltpu.roll(fourth, shift, 1) if shift else fourth
+                here = (lane >= gap) & (lane < gap + 32)
+                lon_out[side, 3 * i + j] = jnp.where(here, moved, field[4 * i + j, :, start:start + 128])
+        return carry
+
+    lax.fori_loop(0, ROWS // 4, tuck, 0)
+
+    pl.semaphore_wait(barrier, len(near_halo + near_line + near_plane))
 
     def send(i, src, dst, to):
         return pltpu.make_async_remote_copy(
@@ -120,33 +145,31 @@
     own_lanes = pl.ds(0, WIDTH)
     left_tile, right_tile = pl.ds(0, 128), pl.ds(WIDTH - 128, 128)
     east_tile, west_tile = pl.ds(EAST, 128), pl.ds(WEST, 128)
-    own_rows = pl.ds(0, ROWS)
     top, bottom = 0, ROWS - 1
     halos = [
         send(0, wcol_out.at[0], wcol_in.at[0], at(0, -1)),
         send(1, wcol_out.at[1], wcol_in.at[1], at(0, 1)),
-        send(2, wc.at[:, top], wc.at[:, SOUTH], at(-1, 0)),
-        send(3, wc.at[:, bottom], wc.at[:, NORTH], at(1, 0)),
+        send(2, wrow_out.at[0], wrow_in.at[0], at(-1, 0)),
+        send(3, wrow_out.at[1], wrow_in.at[1], at(1, 0)),
         send(4, field.at[pl.ds(top, 2), :, own_lanes], field.at[pl.ds(SOUTH, 2), :, own_lanes], at(-1, 0)),
         send(5, field.at[pl.ds(bottom - 1, 2), :, own_lanes], field.at[pl.ds(NORTH - 1, 2), :, own_lanes], at(1, 0)),
-        send(6, field.at[own_rows, :, left_tile], field.at[own_rows, :, east_tile], at(0, -1)),
-        send(7, field.at[own_rows, :, right_tile], field.at[own_rows, :, west_tile], at(0, 1)),
+        send(6, lon_out.at[0], lon_in.at[0], at(0, -1)),
+        send(7, lon_out.at[1], lon_in.at[1], at(0, 1)),
         send(8, field.at[top, :, left_tile], field.at[SOUTH, :, east_tile], at(-1, -1)),
         send(9, field.at[top, :, right_tile], field.at[SOUTH, :, west_tile], at(-1, 1)),
         send(10, field.at[bottom, :, left_tile], field.at[NORTH, :, east_tile], at(1, -1)),
         send(11, field.at[bottom, :, right_tile], field.at[NORTH, :, west_tile], at(1, 1)),
     ]
-    for copy in halos[4:] + halos[:4]:
+    for copy in halos:
         copy.start()
-    for k in near:
-        pl.semaphore_signal(here_sem, inc=1, device_id=line_peer(k % n_line), device_id_type=MESH)
+    for peer in near_line + near_plane:
+        pl.semaphore_signal(here_sem.at[0], inc=1, device_id=peer, device_id_type=MESH)
 
     spread_col = lax.broadcasted_iota(jnp.int32, (COLS, WIDTH), 0)
     spread_lane = lax.broadcasted_iota(jnp.int32, (COLS, WIDTH), 1)
     spread = jnp.where((spread_lane >= spread_col * M) & (spread_lane < spread_col * M + M), 1.0, 0.0).astype(BF16)
 
-    def spread_rows(v, start, rows):
-        w = wc[v, pl.ds(start, rows), :, 0:COLS].reshape(rows * LEV, COLS)
+    def spread_rows(w, v, start, rows):
         a = w.astype(BF16)
         rest = w - a.astype(F32)
         b = rest.astype(BF16)
@@ -159,7 +182,7 @@
         wx[v, pl.ds(start, rows), :, 0:WIDTH] = wide.reshape(rows, LEV, WIDTH)
 
     for v in range(3):
-        spread_rows(v, 0, ROWS)
+        spread_rows(wc[v, :, :, 0:COLS].reshape(ROWS * LEV, COLS), v, 0, ROWS)
 
     def stencil(c, n, s, u, v, w, first, final):
         width = c.shape[1]
@@ -223,13 +246,37 @@
 
     lax.fori_loop(0, OBS, note, 0)
 
-    for i in (0, 1, 6, 7):
+    pl.semaphore_wait(here_sem.at[0], len(near_line + near_plane))
+    for peer in near_line:
+        pl.semaphore_signal(here_sem.at[1], inc=1, device_id=peer, device_id_type=MESH)
+
+    for i in range(4):
         halos[i].wait_recv()
     for v in range(3):
+        for side, start in ((0, SOUTH), (1, NORTH)):
+            spread_rows(wrow_in[side][:, v * COLS:v * COLS + COLS], v, start, 1)
         for side, start in ((0, EAST), (1, WEST)):
             got = wcol_in[side]
             for r in range(ROWS):
                 wx[v, r, :, start:start + 128] = jnp.broadcast_to(got[:, v * ROWS + r:v * ROWS + r + 1], (LEV, 128))
+
+    for i in (6, 7):
+        halos[i].wait_recv()
+
+    def untuck(i, carry):
+        for side, start, free, gap in ((0, EAST, 0, 2 * M), (1, WEST, 32, 0)):
+            fourth = zero_tile
+            for j in range(3):
+                tile = lon_in[side, 3 * i + j]
+                field[4 * i + j, :, start:start + 128] = tile
+                shift = (free + 32 * j - gap) % 128
+                moved = pltpu.roll(tile, shift, 1) if shift else tile
+                here = (lane >= free + 32 * j) & (lane < free + 32 * j + 32)
+                fourth = jnp.where(here, moved, fourth)
+            field[4 * i + 3, :, start:start + 128] = fourth
+        return carry
+
+    lax.fori_loop(0, ROWS // 4, untuck, 0, unroll=2)
 
     def ends_first(r, carry):
         new = west_end(field, r, 0)
@@ -240,11 +287,8 @@
 
     lax.fori_loop(1, ROWS - 1, ends_first, 0, unroll=2)
 
-    for i in (2, 3, 4, 5, 8, 9, 10, 11):
+    for i in (4, 5, 8, 9, 10, 11):
         halos[i].wait_recv()
-    for v in range(3):
-        spread_rows(v, SOUTH, 1)
-        spread_rows(v, NORTH, 1)
     has_north, has_south = lat > 0, lat < n_lat - 1
     field[NORTH] = jnp.where(has_north, field[NORTH], 0.0)
     field[SOUTH] = jnp.where(has_south, field[SOUTH], 0.0)
@@ -268,14 +312,21 @@
     def look(k, carry):
         row, col, lev = cells[0, k] - lat * ROWS, cells[1, k] - lon * COLS, cells[2, k]
         cell = jnp.clip(row * LEV + lev, 0, LEV * ROWS - 1)
-        for t in range(TILES):
-            line = last[t, pl.ds(cell, 1), :]
-            inside = (lane_1 >= col * M - t * 128) & (lane_1 < col * M + M - t * 128)
-            seen[t, pl.ds(k, 1), :] = jnp.where(inside, line, 0.0)
+        first_lane = col * M
+        tile = jnp.clip(first_lane // 128, 0, TILES - 2)
+        lines = []
+        for t in range(2):
+            place = first_lane - (tile + t) * 128
+            inside = (lane_1 >= place) & (lane_1 < place + M)
+            lines.append(jnp.where(inside, last[tile + t, pl.ds(cell, 1), :], 0.0))
+        turn = lax.rem(tile, 3)
+        for t in range(3):
+            one = jnp.where(turn == t, lines[0], 0.0)
+            seen[t, pl.ds(k, 1), :] = jnp.where(turn == (t + 2) % 3, lines[1], one)
         return carry
 
     lax.fori_loop(0, OBS, look, 0, unroll=4)
-    hx = jnp.concatenate([seen[t] + seen[t + 3] + seen[t + 6] for t in range(3)], axis=1)
+    hx = jnp.concatenate([seen[t] for t in range(3)], axis=1)
     hx = hx + pltpu.roll(hx, GROUP // 2, 1)
     hx = hx + pltpu.roll(hx, GROUP // 4, 1)
     hx = hx + pltpu.roll(hx, GROUP // 8, 1)
@@ -317,7 +368,7 @@
 
     wait_all(part1, ar_recv.at[0])
     sum1[...] = pack[core] + jnp.sum(part1[...], axis=0)
-    pl.semaphore_wait(here_sem, len(near))
+    pl.semaphore_wait(here_sem.at[1], len(near_line))
     for j in line_order:
         pltpu.make_async_remote_copy(
             src_ref=sum1, dst_ref=part2.at[j - 1],
@@ -378,6 +429,7 @@
         )
 
     d_high, d_low = diagonal(g_high), diagonal(g_low)
+    done = []
     for g in range(3):
         hi, lo = high[pl.ds(g * 144, 144), :], low[pl.ds(g * 144, 144), :]
         out = (
@@ -386,17 +438,33 @@
             + jnp.dot(hi, d_low, preferred_element_type=F32)
         )
         lanes = pl.ds(g * GROUP, GROUP)
-        tracer_out[:, lanes] = out[0:LEV * ROWS]
-        flux_out[:, lanes] = out[LEV * ROWS:]
+        outs[g] = out
+        done.append(pltpu.make_async_copy(outs.at[g, pl.ds(0, LEV * ROWS)], tracer_out.at[:, lanes], out_sem.at[g]))
+        done.append(pltpu.make_async_copy(outs.at[g, pl.ds(LEV * ROWS, ROWS)], flux_out.at[:, lanes], out_sem.at[3 + g]))
+        for copy in done[-2:]:
+            copy.start()
     for copy in halos:
         copy.wait_send()
     wait_all(part1, ar_send.at[0])
     wait_all(part2, ar_send.at[1])
     swap.wait_send()
+    for copy in done:
+        copy.wait()
+
+
+def hand_on(tracer_in, flux_in, tracer_out, flux_out, sem):
+    copies = [pltpu.make_async_copy(flux_in, flux_out, sem.at[LEV])]
+    for lev in range(LEV):
+        rows = pl.ds(lev * ROWS, ROWS)
+        copies.append(pltpu.make_async_copy(tracer_in.at[rows], tracer_out.at[rows], sem.at[lev]))
+    for copy in copies:
+        copy.start()
+    for copy in copies:
+        copy.wait()
 
 
 def on_device(n_lat, n_lon, tracer, flux, winds, obs_cells, obs_count, obs_value, obs_var):
-    hbm, local = pl.BlockSpec(memory_space=pltpu.HBM), pl.BlockSpec(memory_space=pltpu.VMEM)
+    hbm = pl.BlockSpec(memory_space=pltpu.HBM)
     n_plane, n_line = 2 * n_lat, n_lon // 2
     vmem = pltpu.VMEM
     tracer_out, flux_out = pl.pallas_call(
@@ -406,7 +474,7 @@
             jax.ShapeDtypeStruct((ROWS, WIDTH), F32),
         ),
         in_specs=[hbm] * 7,
-        out_specs=(local, local),
+        out_specs=(hbm, hbm),
         scratch_shapes=[
             vmem((TILES, LEV * ROWS, 128), F32),
             vmem((TILES, ROWS, 128), F32),
@@ -415,11 +483,15 @@
             vmem((ROWS_X, LEV, WIDE), F32),
             vmem((ROWS_X, LEV, WIDE), F32),
             vmem((TILES, LEV * ROWS, 128), F32),
-            vmem((3, ROWS_X, LEV, 128), F32),
+            vmem((3, ROWS, LEV, 128), F32),
             vmem((3, ROWS_X, LEV, WIDE), F32),
             vmem((2, LEV, 128), F32),
             vmem((2, LEV, 128), F32),
-            vmem((TILES, OBS, 128), F32),
+            vmem((2, LEV, 128), F32),
+            vmem((2, LEV, 128), F32),
+            vmem((2, 12, LEV, 128), F32),
+            vmem((2, 12, LEV, 128), F32),
+            vmem((3, OBS, 128), F32),
             vmem((3, OBS, 128), F32),
             vmem((2, 8, 128), F32),
             vmem((n_plane - 1, 8, 128), F32),
@@ -429,16 +501,18 @@
             vmem((8, 128), F32),
             vmem((432, GROUP), BF16),
             vmem((432, GROUP), BF16),
+            vmem((3, 144, GROUP), F32),
             pltpu.SMEM((3, OBS), jnp.int32),
             pltpu.SMEM((1,), jnp.int32),
             pltpu.SMEM((OBS,), F32),
             pltpu.SMEM((OBS,), F32),
             pltpu.SemaphoreType.DMA((5 + 2 * TILES,)),
+            pltpu.SemaphoreType.DMA((6,)),
             pltpu.SemaphoreType.DMA((12,)),
             pltpu.SemaphoreType.DMA((12,)),
             pltpu.SemaphoreType.DMA((3,)),
             pltpu.SemaphoreType.DMA((3,)),
-            pltpu.SemaphoreType.REGULAR,
+            pltpu.SemaphoreType.REGULAR((2,)),
         ],
         compiler_params=pltpu.CompilerParams(
             collective_id=0, has_side_effects=True, vmem_limit_bytes=62 * 1024 * 1024
@@ -448,6 +522,18 @@
         tracer.reshape(LEV * ROWS, WIDTH), flux, winds.reshape(3 * LEV * ROWS, COLS),
         obs_cells.T, obs_count, obs_value, obs_var,
     )
+    tracer_out, flux_out = pl.pallas_call(
+        hand_on,
+        out_shape=(
+            jax.ShapeDtypeStruct((LEV * ROWS, WIDTH), F32),
+            jax.ShapeDtypeStruct((ROWS, WIDTH), F32),
+        ),
+        in_specs=[hbm, hbm],
+        out_specs=(hbm, hbm),
+        scratch_shapes=[pltpu.SemaphoreType.DMA((LEV + 1,))],
+        compiler_params=pltpu.CompilerParams(vmem_limit_bytes=62 * 1024 * 1024),
+        name="hand_on",
+    )(tracer_out, flux_out)
     return tracer_out.reshape(LEV, ROWS, WIDTH), flux_out
 
 

time: 46.8 us -> 65.4 us (1.40)
  Pallas kernels: 42.8 us -> 64 us
  local copies, waits for them, and re-layouts: 2.59 us -> 0 us
    pallas_call x0 -> x1, Pallas kernels: none -> 21.3 us  [on_device(): pl.pallas_call(hand_on, out_shape=(jax.ShapeDtypeStruct((LEV * ROWS, WIDT...]
    unnamed x4 -> x0, local copies, waits for them, and re-layouts: 2.59 us -> none
where the time goes in v3:
time: 65.4 us; the launch traced here: 65.3 us
  Pallas kernels  64 us (98%)
  between operations  1.29 us (2%)
    pallas_call x1, Pallas kernels, on_device(): pl.pallas_call(functools.partial(kernel, n_lat, n_lon), out_shape=(jax.Sh...  42.7 us
    pallas_call x1, Pallas kernels, on_device(): pl.pallas_call(hand_on, out_shape=(jax.ShapeDtypeStruct((LEV * ROWS, WIDT...  21.3 us

profile of v3, /device:TPU:1, one launch (start us, length us, event | category | flops | bytes accessed | tf_op | source)
XLA Modules:
  0.0 65.3 jit_solution(5500110395839156365)
XLA Ops:
  1.3 42.7 %analysis.1 = (f32[128,1152]{1,0:T(8,128)}, f32[16,1152]{1,0:T(8,128)}) custom-call(f32[128,1152]{1,0:T(8,128)} %bitcast.4, f32[16,1152]{1,0:T(8,128)} %flux.1, f32[384,24]{1,0:T(8,128)} %bitcast.5, s32[3,16]{1,0:T(4,128)} %bitcast.6, s32[1]{0:T(128)S(6)} %copy.9.count_in, f32[16]{0:T(128)} %value_in.1, f32[16]{0:T(128)} %var_in.1), custom_call_target="tpu_custom_call" | custom-call | tf_op jit(solution)/shard_map/analysis/pallas_call | solution.py:470
  44.0 21.3 %hand_on.1 = (f32[128,1152]{1,0:T(8,128)}, f32[16,1152]{1,0:T(8,128)}) custom-call(f32[128,1152]{1,0:T(8,128)} %get-tuple-element.6.tracer_in, f32[16,1152]{1,0:T(8,128)} %get-tuple-element.7.flux_in), custom_call_target="tpu_custom_call" | custom-call | tf_op jit(solution)/shard_map/hand_on/pallas_call | solution.py:525

commit v4 on v3

--- a/solution.py
+++ b/solution.py
@@ -22,6 +22,7 @@
 EAST, WEST = WIDTH, WIDTH + 128
 ROWS_X = ROWS + 4
 SOUTH, NORTH = ROWS, ROWS + 3
+CHUNKS = 4
 GROUP = 8 * M
 
 
@@ -98,7 +99,7 @@
             wc[v, r] = wide_winds[pl.ds(v * LEV * ROWS + r, LEV, stride=ROWS), :]
         return carry
 
-    lax.fori_loop(0, ROWS, enter, 0)
+    lax.fori_loop(0, ROWS, enter, 0, unroll=8)
 
     lane = lax.broadcasted_iota(jnp.int32, (LEV, 128), 1)
 
@@ -112,7 +113,7 @@
         return first, final
 
     zero_tile = jnp.zeros((LEV, 128), F32)
-    first, final = lax.fori_loop(0, ROWS, edge, (zero_tile, zero_tile))
+    first, final = lax.fori_loop(0, ROWS, edge, (zero_tile, zero_tile), unroll=True)
     wcol_out[0] = first
     wcol_out[1] = final
     for side, r in ((0, 0), (1, ROWS - 1)):
@@ -132,7 +133,7 @@
                 lon_out[side, 3 * i + j] = jnp.where(here, moved, field[4 * i + j, :, start:start + 128])
         return carry
 
-    lax.fori_loop(0, ROWS // 4, tuck, 0)
+    lax.fori_loop(0, ROWS // 4, tuck, 0, unroll=True)
 
     pl.semaphore_wait(barrier, len(near_halo + near_line + near_plane))
 
@@ -276,7 +277,7 @@
             field[4 * i + 3, :, start:start + 128] = fourth
         return carry
 
-    lax.fori_loop(0, ROWS // 4, untuck, 0, unroll=2)
+    lax.fori_loop(0, ROWS // 4, untuck, 0, unroll=True)
 
     def ends_first(r, carry):
         new = west_end(field, r, 0)
@@ -285,7 +286,7 @@
         mid[r, :, WIDTH - 128:WIDTH + 128] = east_end(field, r, 384)
         return carry
 
-    lax.fori_loop(1, ROWS - 1, ends_first, 0, unroll=2)
+    lax.fori_loop(1, ROWS - 1, ends_first, 0, unroll=7)
 
     for i in (4, 5, 8, 9, 10, 11):
         halos[i].wait_recv()
@@ -305,7 +306,7 @@
         put(r, (TILES - 1,), east_end(mid, r, 256))
         return carry
 
-    lax.fori_loop(2, ROWS - 2, ends_second, 0, unroll=2)
+    lax.fori_loop(2, ROWS - 2, ends_second, 0, unroll=6)
 
     lane_1 = lax.broadcasted_iota(jnp.int32, (1, 128), 1)
 
@@ -325,7 +326,7 @@
             seen[t, pl.ds(k, 1), :] = jnp.where(turn == (t + 2) % 3, lines[1], one)
         return carry
 
-    lax.fori_loop(0, OBS, look, 0, unroll=4)
+    lax.fori_loop(0, OBS, look, 0, unroll=True)
     hx = jnp.concatenate([seen[t] for t in range(3)], axis=1)
     hx = hx + pltpu.roll(hx, GROUP // 2, 1)
     hx = hx + pltpu.roll(hx, GROUP // 4, 1)
@@ -452,14 +453,19 @@
         copy.wait()
 
 
-def hand_on(tracer_in, flux_in, tracer_out, flux_out, sem):
-    copies = [pltpu.make_async_copy(flux_in, flux_out, sem.at[LEV])]
-    for lev in range(LEV):
-        rows = pl.ds(lev * ROWS, ROWS)
-        copies.append(pltpu.make_async_copy(tracer_in.at[rows], tracer_out.at[rows], sem.at[lev]))
-    for copy in copies:
+def hand_on(tracer_in, flux_in, tracer_out, flux_out, held, held_flux, in_sem, out_sem):
+    parts = [(flux_in, held_flux, flux_out)]
+    for i in range(CHUNKS):
+        rows = pl.ds(i * (LEV * ROWS // CHUNKS), LEV * ROWS // CHUNKS)
+        parts.append((tracer_in.at[rows], held.at[rows], tracer_out.at[rows]))
+    into = [pltpu.make_async_copy(src, mid, in_sem.at[i]) for i, (src, mid, _) in enumerate(parts)]
+    out = [pltpu.make_async_copy(mid, dst, out_sem.at[i]) for i, (_, mid, dst) in enumerate(parts)]
+    for copy in into:
         copy.start()
-    for copy in copies:
+    for first, second in zip(into, out):
+        first.wait()
+        second.start()
+    for copy in out:
         copy.wait()
 
 
@@ -530,7 +536,12 @@
         ),
         in_specs=[hbm, hbm],
         out_specs=(hbm, hbm),
-        scratch_shapes=[pltpu.SemaphoreType.DMA((LEV + 1,))],
+        scratch_shapes=[
+            vmem((LEV * ROWS, WIDTH), F32),
+            vmem((ROWS, WIDTH), F32),
+            pltpu.SemaphoreType.DMA((CHUNKS + 1,)),
+            pltpu.SemaphoreType.DMA((CHUNKS + 1,)),
+        ],
         compiler_params=pltpu.CompilerParams(vmem_limit_bytes=62 * 1024 * 1024),
         name="hand_on",
     )(tracer_out, flux_out)

time: 65.4 us -> 43.4 us (0.66)
  Pallas kernels: 64 us -> 41.9 us
    pallas_call x1, Pallas kernels: 21.3 us -> 1.91 us  [on_device(): pl.pallas_call(hand_on, out_shape=(jax.ShapeDtypeStruct((LEV * ROWS, WIDT...]
    pallas_call x1, Pallas kernels: 42.7 us -> 40 us  [on_device(): pl.pallas_call(functools.partial(kernel, n_lat, n_lon), out_shape=(jax.Sh...]
where the time goes in v4:
time: 43.4 us; the launch traced here: 43.2 us
  Pallas kernels  41.9 us (97%)
  between operations  1.29 us (3%)
    pallas_call x1, Pallas kernels, on_device(): pl.pallas_call(functools.partial(kernel, n_lat, n_lon), out_shape=(jax.Sh...  40 us
    pallas_call x1, Pallas kernels, on_device(): pl.pallas_call(hand_on, out_shape=(jax.ShapeDtypeStruct((LEV * ROWS, WIDT...  1.91 us

profile of v4, /device:TPU:1, one launch (start us, length us, event | category | flops | bytes accessed | tf_op | source)
XLA Modules:
  0.0 43.2 jit_solution(11089479886971633116)
XLA Ops:
  1.3 40.0 %analysis.1 = (f32[128,1152]{1,0:T(8,128)}, f32[16,1152]{1,0:T(8,128)}) custom-call(f32[128,1152]{1,0:T(8,128)} %bitcast.4, f32[16,1152]{1,0:T(8,128)} %flux.1, f32[384,24]{1,0:T(8,128)} %bitcast.5, s32[3,16]{1,0:T(4,128)} %bitcast.6, s32[1]{0:T(128)S(6)} %copy.9.count_in, f32[16]{0:T(128)} %value_in.1, f32[16]{0:T(128)} %var_in.1), custom_call_target="tpu_custom_call" | custom-call | tf_op jit(solution)/shard_map/analysis/pallas_call | solution.py:476
  41.3 1.9 %hand_on.1 = (f32[128,1152]{1,0:T(8,128)}, f32[16,1152]{1,0:T(8,128)}) custom-call(f32[128,1152]{1,0:T(8,128)} %get-tuple-element.6.tracer_in, f32[16,1152]{1,0:T(8,128)} %get-tuple-element.7.flux_in), custom_call_target="tpu_custom_call" | custom-call | tf_op jit(solution)/shard_map/hand_on/pallas_call | solution.py:531

commit v5 on v4

--- a/solution.py
+++ b/solution.py
@@ -22,16 +22,15 @@
 EAST, WEST = WIDTH, WIDTH + 128
 ROWS_X = ROWS + 4
 SOUTH, NORTH = ROWS, ROWS + 3
-CHUNKS = 4
 GROUP = 8 * M
 
 
 def kernel(
     n_lat, n_lon,
     tracer, flux, winds, cells_in, count_in, value_in, var_in,
-    tracer_out, flux_out,
+    high_out, low_out, mix_out,
     raw, raw_flux, raw_winds, wide_winds, field, mid, last, wc, wx, wcol_out, wcol_in,
-    wrow_out, wrow_in, lon_out, lon_in, seen, vals, pack, part1, part2, part3, sum1, sum2, high, low, outs,
+    wrow_out, wrow_in, lon_out, lon_in, seen, vals, pack, part1, part2, part3, sum1, sum2, high, low, mix,
     cells, count, value, var, in_sem, out_sem, halo_send, halo_recv, ar_send, ar_recv, here_sem,
 ):
     lat, lon = lax.axis_index("lat"), lax.axis_index("lon")
@@ -364,6 +363,12 @@
             high[rows, lanes] = hi
             low[rows, lanes] = (part - hi.astype(F32)).astype(BF16)
 
+    factors = [
+        pltpu.make_async_copy(high, high_out, out_sem.at[0]), pltpu.make_async_copy(low, low_out, out_sem.at[1]),
+    ]
+    for copy in factors:
+        copy.start()
+
     def wait_all(ref, sem):
         pltpu.make_async_copy(ref, ref, sem).wait()
 
@@ -416,56 +421,62 @@
     mixed = wmean + jnp.sqrt((M - 1.0) / scale) * inverse_now
     mixing = mixed - jnp.sum(mixed, axis=0, keepdims=True) * (1.0 / M) + 1.0 / M
 
-    g_high = mixing.astype(BF16)
-    g_low = (mixing - g_high.astype(F32)).astype(BF16)
-    rep_row = lax.broadcasted_iota(jnp.int32, (M, GROUP), 0)
-    rep_lane = lax.broadcasted_iota(jnp.int32, (M, GROUP), 1)
-    rep = jnp.where(lax.rem(rep_lane, M) == rep_row, 1.0, 0.0).astype(BF16)
-    g_high = jnp.dot(g_high, rep, preferred_element_type=F32)
-    g_low = jnp.dot(g_low, rep, preferred_element_type=F32)
-
-    def diagonal(g):
-        return jnp.concatenate(
-            [jnp.where((rep_lane >= b * M) & (rep_lane < b * M + M), g, 0.0).astype(BF16) for b in range(8)], axis=0
-        )
-
-    d_high, d_low = diagonal(g_high), diagonal(g_low)
-    done = []
-    for g in range(3):
-        hi, lo = high[pl.ds(g * 144, 144), :], low[pl.ds(g * 144, 144), :]
-        out = (
-            jnp.dot(hi, d_high, preferred_element_type=F32)
-            + jnp.dot(lo, d_high, preferred_element_type=F32)
-            + jnp.dot(hi, d_low, preferred_element_type=F32)
-        )
-        lanes = pl.ds(g * GROUP, GROUP)
-        outs[g] = out
-        done.append(pltpu.make_async_copy(outs.at[g, pl.ds(0, LEV * ROWS)], tracer_out.at[:, lanes], out_sem.at[g]))
-        done.append(pltpu.make_async_copy(outs.at[g, pl.ds(LEV * ROWS, ROWS)], flux_out.at[:, lanes], out_sem.at[3 + g]))
-        for copy in done[-2:]:
-            copy.start()
+    mix[...] = mixing
+    result = pltpu.make_async_copy(mix, mix_out, out_sem.at[2])
+    result.start()
     for copy in halos:
         copy.wait_send()
     wait_all(part1, ar_send.at[0])
     wait_all(part2, ar_send.at[1])
     swap.wait_send()
+    for copy in factors:
+        copy.wait()
+    result.wait()
+
+
+def transform(high_in, low_in, mix_in, tracer_out, flux_out, high, low, mix, outs, in_sem, out_sem):
+    mix_copy = pltpu.make_async_copy(mix_in, mix, in_sem.at[6])
+    mix_copy.start()
+    copies = []
+    for g in range(3):
+        rows = pl.ds(g * 144, 144)
+        copies.append(pltpu.make_async_copy(high_in.at[rows], high.at[rows], in_sem.at[2 * g]))
+        copies.append(pltpu.make_async_copy(low_in.at[rows], low.at[rows], in_sem.at[2 * g + 1]))
+    for copy in copies:
+        copy.start()
+
+    rep_row = lax.broadcasted_iota(jnp.int32, (M, GROUP), 0)
+    rep_lane = lax.broadcasted_iota(jnp.int32, (M, GROUP), 1)
+    rep = jnp.where(lax.rem(rep_lane, M) == rep_row, 1.0, 0.0).astype(BF16)
+    mix_copy.wait()
+    mixing = mix[...]
+    g_high = mixing.astype(BF16)
+    g_low = (mixing - g_high.astype(F32)).astype(BF16)
+    g_high = jnp.dot(g_high, rep, preferred_element_type=F32)
+    g_low = jnp.dot(g_low, rep, preferred_element_type=F32)
+
+    def diagonal(g):
+        return jnp.concatenate(
+            [jnp.where((rep_lane >= b * M) & (rep_lane < b * M + M), g, 0.0).astype(BF16) for b in range(8)], axis=0
+        )
+
+    d_high, d_low = diagonal(g_high), diagonal(g_low)
+    done = []
+    for g in range(3):
+        for copy in copies[2 * g:2 * g + 2]:
+            copy.wait()
+        hi, lo = high[pl.ds(g * 144, 144), :], low[pl.ds(g * 144, 144), :]
+        outs[g] = (
+            jnp.dot(hi, d_high, preferred_element_type=F32)
+            + jnp.dot(lo, d_high, preferred_element_type=F32)
+            + jnp.dot(hi, d_low, preferred_element_type=F32)
+        )
+        lanes = pl.ds(g * GROUP, GROUP)
+        done.append(pltpu.make_async_copy(outs.at[g, pl.ds(0, LEV * ROWS)], tracer_out.at[:, lanes], out_sem.at[g]))
+        done.append(pltpu.make_async_copy(outs.at[g, pl.ds(LEV * ROWS, ROWS)], flux_out.at[:, lanes], out_sem.at[3 + g]))
+        for copy in done[-2:]:
+            copy.start()
     for copy in done:
-        copy.wait()
-
-
-def hand_on(tracer_in, flux_in, tracer_out, flux_out, held, held_flux, in_sem, out_sem):
-    parts = [(flux_in, held_flux, flux_out)]
-    for i in range(CHUNKS):
-        rows = pl.ds(i * (LEV * ROWS // CHUNKS), LEV * ROWS // CHUNKS)
-        parts.append((tracer_in.at[rows], held.at[rows], tracer_out.at[rows]))
-    into = [pltpu.make_async_copy(src, mid, in_sem.at[i]) for i, (src, mid, _) in enumerate(parts)]
-    out = [pltpu.make_async_copy(mid, dst, out_sem.at[i]) for i, (_, mid, dst) in enumerate(parts)]
-    for copy in into:
-        copy.start()
-    for first, second in zip(into, out):
-        first.wait()
-        second.start()
-    for copy in out:
         copy.wait()
 
 
@@ -473,14 +484,15 @@
     hbm = pl.BlockSpec(memory_space=pltpu.HBM)
     n_plane, n_line = 2 * n_lat, n_lon // 2
     vmem = pltpu.VMEM
-    tracer_out, flux_out = pl.pallas_call(
+    high, low, mixing = pl.pallas_call(
         functools.partial(kernel, n_lat, n_lon),
         out_shape=(
-            jax.ShapeDtypeStruct((LEV * ROWS, WIDTH), F32),
-            jax.ShapeDtypeStruct((ROWS, WIDTH), F32),
+            jax.ShapeDtypeStruct((432, GROUP), BF16),
+            jax.ShapeDtypeStruct((432, GROUP), BF16),
+            jax.ShapeDtypeStruct((M, M), F32),
         ),
         in_specs=[hbm] * 7,
-        out_specs=(hbm, hbm),
+        out_specs=(hbm, hbm, hbm),
         scratch_shapes=[
             vmem((TILES, LEV * ROWS, 128), F32),
             vmem((TILES, ROWS, 128), F32),
@@ -507,13 +519,13 @@
             vmem((8, 128), F32),
             vmem((432, GROUP), BF16),
             vmem((432, GROUP), BF16),
-            vmem((3, 144, GROUP), F32),
+            vmem((M, M), F32),
             pltpu.SMEM((3, OBS), jnp.int32),
             pltpu.SMEM((1,), jnp.int32),
             pltpu.SMEM((OBS,), F32),
             pltpu.SMEM((OBS,), F32),
             pltpu.SemaphoreType.DMA((5 + 2 * TILES,)),
-            pltpu.SemaphoreType.DMA((6,)),
+            pltpu.SemaphoreType.DMA((3,)),
             pltpu.SemaphoreType.DMA((12,)),
             pltpu.SemaphoreType.DMA((12,)),
             pltpu.SemaphoreType.DMA((3,)),
@@ -529,22 +541,24 @@
         obs_cells.T, obs_count, obs_value, obs_var,
     )
     tracer_out, flux_out = pl.pallas_call(
-        hand_on,
+        transform,
         out_shape=(
             jax.ShapeDtypeStruct((LEV * ROWS, WIDTH), F32),
             jax.ShapeDtypeStruct((ROWS, WIDTH), F32),
         ),
-        in_specs=[hbm, hbm],
+        in_specs=[hbm] * 3,
         out_specs=(hbm, hbm),
         scratch_shapes=[
-            vmem((LEV * ROWS, WIDTH), F32),
-            vmem((ROWS, WIDTH), F32),
-            pltpu.SemaphoreType.DMA((CHUNKS + 1,)),
-            pltpu.SemaphoreType.DMA((CHUNKS + 1,)),
+            vmem((432, GROUP), BF16),
+            vmem((432, GROUP), BF16),
+            vmem((M, M), F32),
+            vmem((3, 144, GROUP), F32),
+            pltpu.SemaphoreType.DMA((7,)),
+            pltpu.SemaphoreType.DMA((6,)),
         ],
         compiler_params=pltpu.CompilerParams(vmem_limit_bytes=62 * 1024 * 1024),
-        name="hand_on",
-    )(tracer_out, flux_out)
+        name="transform",
+    )(high, low, mixing)
     return tracer_out.reshape(LEV, ROWS, WIDTH), flux_out
 
 

time: 43.4 us -> 43.4 us (level)
    pallas_call x1, Pallas kernels: 40 us -> 38.9 us  [on_device(): pl.pallas_call(functools.partial(kernel, n_lat, n_lon), out_shape=(jax.Sh...]
    pallas_call x1, Pallas kernels: 1.91 us -> 2.96 us  [on_device(): pl.pallas_call(transform, out_shape=(jax.ShapeDtypeStruct((LEV * ROWS, WI...]
where the time goes in v5:
time: 43.4 us; the launch traced here: 43.2 us
  Pallas kernels  41.9 us (97%)
  between operations  1.29 us (3%)
    pallas_call x1, Pallas kernels, on_device(): pl.pallas_call(functools.partial(kernel, n_lat, n_lon), out_shape=(jax.Sh...  38.9 us
    pallas_call x1, Pallas kernels, on_device(): pl.pallas_call(transform, out_shape=(jax.ShapeDtypeStruct((LEV * ROWS, WI...  2.96 us

profile of v5, /device:TPU:1, one launch (start us, length us, event | category | flops | bytes accessed | tf_op | source)
XLA Modules:
  0.0 43.2 jit_solution(17601286956513489416)
XLA Ops:
  1.3 38.9 %analysis.1 = (bf16[432,384]{1,0:T(8,128)(2,1)}, bf16[432,384]{1,0:T(8,128)(2,1)}, f32[48,48]{1,0:T(8,128)}) custom-call(f32[128,1152]{1,0:T(8,128)} %bitcast.4, f32[16,1152]{1,0:T(8,128)} %flux.1, f32[384,24]{1,0:T(8,128)} %bitcast.5, s32[3,16]{1,0:T(4,128)} %bitcast.6, s32[1]{0:T(128)S(6)} %copy.9.count_in, f32[16]{0:T(128)} %value_in.1, f32[16]{0:T(128)} %var_in.1), custom_call_target="tpu_custom_call" | custom-call | tf_op jit(solution)/shard_map/analysis/pallas_call | solution.py:487
  40.2 3.0 %transform.1 = (f32[128,1152]{1,0:T(8,128)}, f32[16,1152]{1,0:T(8,128)}) custom-call(bf16[432,384]{1,0:T(8,128)(2,1)} %get-tuple-element.7.high_in, bf16[432,384]{1,0:T(8,128)(2,1)} %get-tuple-element.8.low_in, f32[48,48]{1,0:T(8,128)} %get-tuple-element.9.mix_in), custom_call_target="tpu_custom_call" | custom-call | tf_op jit(solution)/shard_map/transform/pallas_call | solution.py:543

commit v6 on v5

--- a/solution.py
+++ b/solution.py
@@ -245,6 +245,11 @@
         return carry
 
     lax.fori_loop(0, OBS, note, 0)
+    spots = []
+    for k in range(OBS):
+        row, first_lane, lev = cells[0, k] - lat * ROWS, (cells[1, k] - lon * COLS) * M, cells[2, k]
+        tile = jnp.clip(first_lane // 128, 0, TILES - 2)
+        spots.append((jnp.clip(row * LEV + lev, 0, LEV * ROWS - 1), tile, first_lane - tile * 128, lax.rem(tile, 3)))
 
     pl.semaphore_wait(here_sem.at[0], len(near_line + near_plane))
     for peer in near_line:
@@ -309,23 +314,14 @@
 
     lane_1 = lax.broadcasted_iota(jnp.int32, (1, 128), 1)
 
-    def look(k, carry):
-        row, col, lev = cells[0, k] - lat * ROWS, cells[1, k] - lon * COLS, cells[2, k]
-        cell = jnp.clip(row * LEV + lev, 0, LEV * ROWS - 1)
-        first_lane = col * M
-        tile = jnp.clip(first_lane // 128, 0, TILES - 2)
+    for k, (cell, tile, start, turn) in enumerate(spots):
         lines = []
         for t in range(2):
-            place = first_lane - (tile + t) * 128
-            inside = (lane_1 >= place) & (lane_1 < place + M)
+            inside = (lane_1 >= start - t * 128) & (lane_1 < start - t * 128 + M)
             lines.append(jnp.where(inside, last[tile + t, pl.ds(cell, 1), :], 0.0))
-        turn = lax.rem(tile, 3)
         for t in range(3):
             one = jnp.where(turn == t, lines[0], 0.0)
-            seen[t, pl.ds(k, 1), :] = jnp.where(turn == (t + 2) % 3, lines[1], one)
-        return carry
-
-    lax.fori_loop(0, OBS, look, 0, unroll=True)
+            seen[t, k:k + 1, :] = jnp.where(turn == (t + 2) % 3, lines[1], one)
     hx = jnp.concatenate([seen[t] for t in range(3)], axis=1)
     hx = hx + pltpu.roll(hx, GROUP // 2, 1)
     hx = hx + pltpu.roll(hx, GROUP // 4, 1)
@@ -462,15 +458,17 @@
 
     d_high, d_low = diagonal(g_high), diagonal(g_low)
     done = []
+    for copy in copies:
+        copy.wait()
+    for n, (k0, k1) in enumerate(((0, 256), (0, 384), (128, 384))):
+        cols = slice(n * 128, n * 128 + 128)
+        w_h, w_l = d_high[k0:k1, cols], d_low[k0:k1, cols]
+        w = jnp.concatenate([w_h, w_l], axis=1)
+        both = jnp.dot(high[:, k0:k1], w, preferred_element_type=F32)
+        res = both[:, 0:128] + both[:, 128:256] + jnp.dot(low[:, k0:k1], w_h, preferred_element_type=F32)
+        for g in range(3):
+            outs[g, :, cols] = res[g * 144:(g + 1) * 144]
     for g in range(3):
-        for copy in copies[2 * g:2 * g + 2]:
-            copy.wait()
-        hi, lo = high[pl.ds(g * 144, 144), :], low[pl.ds(g * 144, 144), :]
-        outs[g] = (
-            jnp.dot(hi, d_high, preferred_element_type=F32)
-            + jnp.dot(lo, d_high, preferred_element_type=F32)
-            + jnp.dot(hi, d_low, preferred_element_type=F32)
-        )
         lanes = pl.ds(g * GROUP, GROUP)
         done.append(pltpu.make_async_copy(outs.at[g, pl.ds(0, LEV * ROWS)], tracer_out.at[:, lanes], out_sem.at[g]))
         done.append(pltpu.make_async_copy(outs.at[g, pl.ds(LEV * ROWS, ROWS)], flux_out.at[:, lanes], out_sem.at[3 + g]))

time: 43.4 us -> 43 us (level)
  no operation moved by 1% of the time
where the time goes in v6:
time: 43 us; the launch traced here: 42.8 us
  Pallas kernels  41.5 us (97%)
  between operations  1.29 us (3%)
    pallas_call x1, Pallas kernels, on_device(): pl.pallas_call(functools.partial(kernel, n_lat, n_lon), out_shape=(jax.Sh...  38.8 us
    pallas_call x1, Pallas kernels, on_device(): pl.pallas_call(transform, out_shape=(jax.ShapeDtypeStruct((LEV * ROWS, WI...  2.73 us

profile of v6, /device:TPU:1, one launch (start us, length us, event | category | flops | bytes accessed | tf_op | source)
XLA Modules:
  0.0 42.8 jit_solution(10322907787392724968)
XLA Ops:
  1.3 38.8 %analysis.1 = (bf16[432,384]{1,0:T(8,128)(2,1)}, bf16[432,384]{1,0:T(8,128)(2,1)}, f32[48,48]{1,0:T(8,128)}) custom-call(f32[128,1152]{1,0:T(8,128)} %bitcast.4, f32[16,1152]{1,0:T(8,128)} %flux.1, f32[384,24]{1,0:T(8,128)} %bitcast.5, s32[3,16]{1,0:T(4,128)} %bitcast.6, s32[1]{0:T(128)S(6)} %copy.9.count_in, f32[16]{0:T(128)} %value_in.1, f32[16]{0:T(128)} %var_in.1), custom_call_target="tpu_custom_call" | custom-call | tf_op jit(solution)/shard_map/analysis/pallas_call | solution.py:485
  40.1 2.7 %transform.1 = (f32[128,1152]{1,0:T(8,128)}, f32[16,1152]{1,0:T(8,128)}) custom-call(bf16[432,384]{1,0:T(8,128)(2,1)} %get-tuple-element.7.high_in, bf16[432,384]{1,0:T(8,128)(2,1)} %get-tuple-element.8.low_in, f32[48,48]{1,0:T(8,128)} %get-tuple-element.9.mix_in), custom_call_target="tpu_custom_call" | custom-call | tf_op jit(solution)/shard_map/transform/pallas_call | solution.py:541

commit v7 on v6

--- a/solution.py
+++ b/solution.py
@@ -403,10 +403,12 @@
         return jnp.dot(a, b, precision=HP, preferred_element_type=F32)
 
     system = (M - 1.0) * eye + gram
-    scale = jnp.sqrt(jnp.sum(system * system, keepdims=True))
+    square = dot(system, system)
+    norm2 = jnp.sum(system * system, keepdims=True)
+    scale = jnp.sqrt(norm2)
     root_now = system / scale
     factor = 0.5 * (3.0 * eye - root_now)
-    root_now, inverse_now = dot(root_now, factor), factor
+    root_now, inverse_now = 1.5 * root_now - 0.5 * (square / norm2), factor
     for step in range(1, NS_ITERS):
         factor = 0.5 * (3.0 * eye - dot(inverse_now, root_now))
         if step < NS_ITERS - 1:
@@ -467,12 +469,14 @@
         both = jnp.dot(high[:, k0:k1], w, preferred_element_type=F32)
         res = both[:, 0:128] + both[:, 128:256] + jnp.dot(low[:, k0:k1], w_h, preferred_element_type=F32)
         for g in range(3):
-            outs[g, :, cols] = res[g * 144:(g + 1) * 144]
-    for g in range(3):
-        lanes = pl.ds(g * GROUP, GROUP)
-        done.append(pltpu.make_async_copy(outs.at[g, pl.ds(0, LEV * ROWS)], tracer_out.at[:, lanes], out_sem.at[g]))
-        done.append(pltpu.make_async_copy(outs.at[g, pl.ds(LEV * ROWS, ROWS)], flux_out.at[:, lanes], out_sem.at[3 + g]))
-        for copy in done[-2:]:
+            outs[g * 3 + n] = res[g * 144:(g + 1) * 144]
+        for t in range(n, TILES, 3):
+            lanes = pl.ds(t * 128, 128)
+            done.append(pltpu.make_async_copy(outs.at[t, pl.ds(0, LEV * ROWS)], tracer_out.at[:, lanes], out_sem.at[t]))
+            done.append(
+                pltpu.make_async_copy(outs.at[t, pl.ds(LEV * ROWS, ROWS)], flux_out.at[:, lanes], out_sem.at[TILES + t])
+            )
+        for copy in done[-6:]:
             copy.start()
     for copy in done:
         copy.wait()
@@ -550,9 +554,9 @@
             vmem((432, GROUP), BF16),
             vmem((432, GROUP), BF16),
             vmem((M, M), F32),
-            vmem((3, 144, GROUP), F32),
+            vmem((TILES, 144, 128), F32),
             pltpu.SemaphoreType.DMA((7,)),
-            pltpu.SemaphoreType.DMA((6,)),
+            pltpu.SemaphoreType.DMA((2 * TILES,)),
         ],
         compiler_params=pltpu.CompilerParams(vmem_limit_bytes=62 * 1024 * 1024),
         name="transform",

time: 43 us -> 42.8 us (level)
  no operation moved by 1% of the time
where the time goes in v7:
time: 42.8 us; the launch traced here: 42.6 us
  Pallas kernels  41.4 us (97%)
  between operations  1.29 us (3%)
    pallas_call x1, Pallas kernels, on_device(): pl.pallas_call(functools.partial(kernel, n_lat, n_lon), out_shape=(jax.Sh...  38.7 us
    pallas_call x1, Pallas kernels, on_device(): pl.pallas_call(transform, out_shape=(jax.ShapeDtypeStruct((LEV * ROWS, WI...  2.69 us

profile of v7, /device:TPU:1, one launch (start us, length us, event | category | flops | bytes accessed | tf_op | source)
XLA Modules:
  0.0 42.6 jit_solution(11672098691696910190)
XLA Ops:
  1.3 38.7 %analysis.1 = (bf16[432,384]{1,0:T(8,128)(2,1)}, bf16[432,384]{1,0:T(8,128)(2,1)}, f32[48,48]{1,0:T(8,128)}) custom-call(f32[128,1152]{1,0:T(8,128)} %bitcast.4, f32[16,1152]{1,0:T(8,128)} %flux.1, f32[384,24]{1,0:T(8,128)} %bitcast.5, s32[3,16]{1,0:T(4,128)} %bitcast.6, s32[1]{0:T(128)S(6)} %copy.9.count_in, f32[16]{0:T(128)} %value_in.1, f32[16]{0:T(128)} %var_in.1), custom_call_target="tpu_custom_call" | custom-call | tf_op jit(solution)/shard_map/analysis/pallas_call | solution.py:489
  39.9 2.7 %transform.1 = (f32[128,1152]{1,0:T(8,128)}, f32[16,1152]{1,0:T(8,128)}) custom-call(bf16[432,384]{1,0:T(8,128)(2,1)} %get-tuple-element.7.high_in, bf16[432,384]{1,0:T(8,128)(2,1)} %get-tuple-element.8.low_in, f32[48,48]{1,0:T(8,128)} %get-tuple-element.9.mix_in), custom_call_target="tpu_custom_call" | custom-call | tf_op jit(solution)/shard_map/transform/pallas_call | solution.py:545

commit v8 on v7

--- a/solution.py
+++ b/solution.py
@@ -249,7 +249,7 @@
     for k in range(OBS):
         row, first_lane, lev = cells[0, k] - lat * ROWS, (cells[1, k] - lon * COLS) * M, cells[2, k]
         tile = jnp.clip(first_lane // 128, 0, TILES - 2)
-        spots.append((jnp.clip(row * LEV + lev, 0, LEV * ROWS - 1), tile, first_lane - tile * 128, lax.rem(tile, 3)))
+        spots.append((jnp.clip(row * LEV + lev, 0, LEV * ROWS - 1), tile, (256 - first_lane + tile * 128) & 255))
 
     pl.semaphore_wait(here_sem.at[0], len(near_line + near_plane))
     for peer in near_line:
@@ -312,33 +312,23 @@
 
     lax.fori_loop(2, ROWS - 2, ends_second, 0, unroll=6)
 
-    lane_1 = lax.broadcasted_iota(jnp.int32, (1, 128), 1)
-
-    for k, (cell, tile, start, turn) in enumerate(spots):
-        lines = []
-        for t in range(2):
-            inside = (lane_1 >= start - t * 128) & (lane_1 < start - t * 128 + M)
-            lines.append(jnp.where(inside, last[tile + t, pl.ds(cell, 1), :], 0.0))
-        for t in range(3):
-            one = jnp.where(turn == t, lines[0], 0.0)
-            seen[t, k:k + 1, :] = jnp.where(turn == (t + 2) % 3, lines[1], one)
-    hx = jnp.concatenate([seen[t] for t in range(3)], axis=1)
-    hx = hx + pltpu.roll(hx, GROUP // 2, 1)
-    hx = hx + pltpu.roll(hx, GROUP // 4, 1)
-    hx = hx + pltpu.roll(hx, GROUP // 8, 1)
+
+    for k, (cell, tile, shift) in enumerate(spots):
+        line = jnp.concatenate([last[tile, pl.ds(cell, 1), :], last[tile + 1, pl.ds(cell, 1), :]], axis=1)
+        seen[k:k + 1, :] = pltpu.roll(line, shift, 1)[:, 0:128]
+    hx = seen[...]
     lane_o = lax.broadcasted_iota(jnp.int32, (OBS, 128), 1)
-    hbar = jnp.sum(jnp.where(lane_o < M, hx[:, 0:128], 0.0), axis=1, keepdims=True) * (1.0 / M)
+    hbar = jnp.sum(jnp.where(lane_o < M, hx, 0.0), axis=1, keepdims=True) * (1.0 / M)
     y = hx - hbar
     q = vals[0] / vals[1]
     d = vals[2] - hbar
 
-    y0 = y[:, 0:128]
-    y32 = pltpu.roll(y, 32, 1)[:, 0:128]
+    y0, y32, y48 = y, pltpu.roll(y, 32, 1), pltpu.roll(y, 48, 1)
     w0 = jnp.where(lane_o < 48, y0, jnp.where(lane_o == 96, d, 0.0))
     w1 = jnp.where((lane_o >= 48) & (lane_o < 80), y32, jnp.where(lane_o == 97, d, 0.0))
-    w2 = jnp.where((lane_o >= 80) & (lane_o < 96), y0, jnp.where(lane_o == 98, d, 0.0))
-    l1 = pltpu.roll(y, GROUP - 16, 1)[:, 0:128]
-    l2 = pltpu.roll(y, GROUP - 32, 1)[:, 0:128]
+    w2 = jnp.where((lane_o >= 80) & (lane_o < 96), y48, jnp.where(lane_o == 98, d, 0.0))
+    l1 = pltpu.roll(y, 128 - 16, 1)
+    l2 = pltpu.roll(y, 128 - 32, 1)
     lhs = jnp.concatenate([q * y0, q * l1, q * l2], axis=0)
     rhs = jnp.concatenate([w0, w1, w2], axis=0)
     packed = lax.dot_general(lhs, rhs, (((0,), (0,)), ((), ())), precision=HP, preferred_element_type=F32)[0:16]
@@ -511,7 +501,7 @@
             vmem((2, LEV, 128), F32),
             vmem((2, 12, LEV, 128), F32),
             vmem((2, 12, LEV, 128), F32),
-            vmem((3, OBS, 128), F32),
+            vmem((OBS, 128), F32),
             vmem((3, OBS, 128), F32),
             vmem((2, 8, 128), F32),
             vmem((n_plane - 1, 8, 128), F32),

time: 42.8 us -> 42.6 us (level)
  no operation moved by 1% of the time
where the time goes in v8:
time: 42.6 us; the launch traced here: 42.5 us
  Pallas kernels  41.2 us (97%)
  between operations  1.29 us (3%)
    pallas_call x1, Pallas kernels, on_device(): pl.pallas_call(functools.partial(kernel, n_lat, n_lon), out_shape=(jax.Sh...  38.5 us
    pallas_call x1, Pallas kernels, on_device(): pl.pallas_call(transform, out_shape=(jax.ShapeDtypeStruct((LEV * ROWS, WI...  2.69 us

profile of v8, /device:TPU:1, one launch (start us, length us, event | category | flops | bytes accessed | tf_op | source)
XLA Modules:
  0.0 42.5 jit_solution(11441754438293900611)
XLA Ops:
  1.3 38.5 %analysis.1 = (bf16[432,384]{1,0:T(8,128)(2,1)}, bf16[432,384]{1,0:T(8,128)(2,1)}, f32[48,48]{1,0:T(8,128)}) custom-call(f32[128,1152]{1,0:T(8,128)} %bitcast.4, f32[16,1152]{1,0:T(8,128)} %flux.1, f32[384,24]{1,0:T(8,128)} %bitcast.5, s32[3,16]{1,0:T(4,128)} %bitcast.6, s32[1]{0:T(128)S(6)} %copy.9.count_in, f32[16]{0:T(128)} %value_in.1, f32[16]{0:T(128)} %var_in.1), custom_call_target="tpu_custom_call" | custom-call | tf_op jit(solution)/shard_map/analysis/pallas_call | solution.py:479
  39.8 2.7 %transform.1 = (f32[128,1152]{1,0:T(8,128)}, f32[16,1152]{1,0:T(8,128)}) custom-call(bf16[432,384]{1,0:T(8,128)(2,1)} %get-tuple-element.7.high_in, bf16[432,384]{1,0:T(8,128)(2,1)} %get-tuple-element.8.low_in, f32[48,48]{1,0:T(8,128)} %get-tuple-element.9.mix_in), custom_call_target="tpu_custom_call" | custom-call | tf_op jit(solution)/shard_map/transform/pallas_call | solution.py:535

commit v9 on v8

--- a/solution.py
+++ b/solution.py
@@ -381,11 +381,20 @@
     u0 = jnp.where(lane_p < 48, total, 0.0)
     u1 = jnp.where((lane_p >= 16) & (lane_p < 48), pltpu.roll(total, 128 - 32, 1), 0.0)
     u2 = jnp.where((lane_p >= 32) & (lane_p < 48), pltpu.roll(total, 128 - 48, 1), 0.0)
-    upper = jnp.concatenate([u0, u1, u2, jnp.zeros((80, 128), F32)], axis=0)
-    flipped = upper.T
+    flipped = total.T
     row_s = lax.broadcasted_iota(jnp.int32, (M, M), 0)
     col_s = lax.broadcasted_iota(jnp.int32, (M, M), 1)
-    gram = jnp.where(row_s // 16 > col_s // 16, flipped[0:M, 0:M], upper[0:M, 0:M])
+    upper = jnp.concatenate([u0, u1, u2], axis=0)[:, 0:M]
+    corner = jnp.concatenate([flipped[32:48], flipped[64:80]], axis=1)
+    lower = jnp.concatenate(
+        [
+            jnp.zeros((16, M), F32),
+            jnp.concatenate([flipped[16:32], jnp.zeros((16, 32), F32)], axis=1),
+            jnp.concatenate([corner, jnp.zeros((16, 16), F32)], axis=1),
+        ],
+        axis=0,
+    )
+    gram = upper + lower
     proj = jnp.concatenate([total[:, 96:97], total[:, 97:98], total[:, 98:99]], axis=0)
     eye = jnp.where(row_s == col_s, 1.0, 0.0)
 

time: 42.6 us -> 42.7 us (level)
  no operation moved by 1% of the time
where the time goes in v9:
time: 42.7 us; the launch traced here: 42.5 us
  Pallas kernels  41.2 us (96%)
  between operations  1.29 us (3%)
    pallas_call x1, Pallas kernels, on_device(): pl.pallas_call(functools.partial(kernel, n_lat, n_lon), out_shape=(jax.Sh...  38.5 us
    pallas_call x1, Pallas kernels, on_device(): pl.pallas_call(transform, out_shape=(jax.ShapeDtypeStruct((LEV * ROWS, WI...  2.7 us

profile of v9, /device:TPU:1, one launch (start us, length us, event | category | flops | bytes accessed | tf_op | source)
XLA Modules:
  0.0 42.5 jit_solution(11625744046194013507)
XLA Ops:
  1.3 38.5 %analysis.1 = (bf16[432,384]{1,0:T(8,128)(2,1)}, bf16[432,384]{1,0:T(8,128)(2,1)}, f32[48,48]{1,0:T(8,128)}) custom-call(f32[128,1152]{1,0:T(8,128)} %bitcast.4, f32[16,1152]{1,0:T(8,128)} %flux.1, f32[384,24]{1,0:T(8,128)} %bitcast.5, s32[3,16]{1,0:T(4,128)} %bitcast.6, s32[1]{0:T(128)S(6)} %copy.9.count_in, f32[16]{0:T(128)} %value_in.1, f32[16]{0:T(128)} %var_in.1), custom_call_target="tpu_custom_call" | custom-call | tf_op jit(solution)/shard_map/analysis/pallas_call | solution.py:488
  39.8 2.7 %transform.1 = (f32[128,1152]{1,0:T(8,128)}, f32[16,1152]{1,0:T(8,128)}) custom-call(bf16[432,384]{1,0:T(8,128)(2,1)} %get-tuple-element.7.high_in, bf16[432,384]{1,0:T(8,128)(2,1)} %get-tuple-element.8.low_in, f32[48,48]{1,0:T(8,128)} %get-tuple-element.9.mix_in), custom_call_target="tpu_custom_call" | custom-call | tf_op jit(solution)/shard_map/transform/pallas_call | solution.py:544
